TPU v7x, 32 devices: a whole 2x2x4 slice. The times are simulated.
32 devices in a mesh: dp: 8 (over y, x, core), mp: 4 (over z).
Axes of the slice: x: 2, y: 2, z: 4, core: 2. Of those that a mesh axis runs over, the one named last changes fastest.
Arguments:
- prefix_in: bfloat16 [8, 512, 2048], P('dp', 'mp'), may hold values from -6 to 6
- action_in: bfloat16 [8, 50, 1024], P('dp'), may hold values from -6 to 6
- prefix_len: int32 [8], P('dp'), may hold values from 448 to 512, as said below
- action_count: int32 [8], P('dp'), may hold values from 25 to 50, as said below
- loss_weight: int32 [8], P('dp'), may hold values from 1 to 4
- prefix_gains: bfloat16 [2048, 2], P(('dp', 'mp')), may hold values from 0.099609375 to 1.8984375
- action_gains: bfloat16 [1024, 2], P(('dp', 'mp')), may hold values from 0.099609375 to 1.8984375
- prefix_qkv: bfloat16 [2048, 2560], P(('dp', 'mp')), may hold values from -0.125 to 0.125
- prefix_out_proj: bfloat16 [2048, 2048], P(('dp', 'mp')), may hold values from -0.75 to 0.75
- action_qkv: bfloat16 [1024, 2560], P(('dp', 'mp')), may hold values from -0.1875 to 0.1875
- action_out_proj: bfloat16 [2048, 1024], P(('dp', 'mp')), may hold values from -0.75 to 0.75
- prefix_gate_up: bfloat16 [2, 2048, 16384], P(None, 'dp', 'mp'), may hold values from -0.125 to 0.125
- prefix_down: bfloat16 [16384, 2048], P('mp', 'dp'), may hold values from -0.09375 to 0.09375
- action_gate_up: bfloat16 [2, 1024, 4096], P(None, 'dp', 'mp'), may hold values from -0.1875 to 0.1875
- action_down: bfloat16 [4096, 1024], P('mp', 'dp'), may hold values from -0.1875 to 0.1875
- prefix_cot: bfloat16 [8, 512, 2048], P('dp', 'mp'), may hold values from -6 to 6
- action_cot: bfloat16 [8, 50, 1024], P('dp'), may hold values from -6 to 6
Outputs:
- prefix_out: bfloat16 [8, 512, 2048], P('dp', 'mp')
- action_out: bfloat16 [8, 50, 1024], P('dp')
- prefix_in_grad: float32 [8, 512, 2048], P('dp', 'mp')
- action_in_grad: float32 [8, 50, 1024], P('dp')
- prefix_gains_grad: float32 [2048, 2], P(('dp', 'mp'))
- action_gains_grad: float32 [1024, 2], P(('dp', 'mp'))
- prefix_qkv_grad: float32 [2048, 2560], P(('dp', 'mp'))
- prefix_out_proj_grad: float32 [2048, 2048], P(('dp', 'mp'))
- action_qkv_grad: float32 [1024, 2560], P(('dp', 'mp'))
- action_out_proj_grad: float32 [2048, 1024], P(('dp', 'mp'))
- prefix_gate_up_grad: float32 [2, 2048, 16384], P(None, 'dp', 'mp')
- prefix_down_grad: float32 [16384, 2048], P('mp', 'dp')
- action_gate_up_grad: float32 [2, 1024, 4096], P(None, 'dp', 'mp')
- action_down_grad: float32 [4096, 1024], P('mp', 'dp')
Inputs may be any that keep to these rules, and one draw needn't show every extreme that they name: `prefix_len`: some item counts all 512 positions in every draw. `action_count`: some item counts all 50 action tokens in every draw.
All inputs are finite; a program needn't handle non-finite values.
Results may differ from a plain program's by a relative error of at most 0.02.
Values may be sent and summed in bfloat16 or wider, within the bound.
No kernel may reach another device: no remote copies, remote signals or barrier semaphores. Data moves between devices by JAX's collectives and lax.ppermute only.
A program may use at most 256 MiB of HBM per device.

v0:
```python
import math

import jax
import jax.numpy as jnp
from jax import lax
from jax.sharding import PartitionSpec as P

HEADS = 8
HD = 256


EPS = 1e-06


def normed(values, gain):
    scale = lax.rsqrt(jnp.mean(values * values, axis=-1, keepdims=True) + EPS)
    return values * scale * gain


def geglu(gate, up_part):
    return jax.nn.gelu(gate, approximate=True) * up_part


def project(left, right):
    return jnp.einsum("itk,kn->itn", left, right, preferred_element_type=jnp.float32)


def project_back(left, right):
    return jnp.einsum("itn,kn->itk", left, right, preferred_element_type=jnp.float32)


def outer_sum(left, right):
    return jnp.einsum("itk,itn->kn", left, right, preferred_element_type=jnp.float32)


def scores_of(query, keys, keep):
    heads = query.reshape(query.shape[0], query.shape[1], HEADS, HD)
    raw = jnp.einsum("ithd,iud->ihtu", heads, keys[..., :HD], preferred_element_type=jnp.float32)
    return jnp.where(keep[:, None, None, :], raw * (1.0 / math.sqrt(HD)), -1e30)


def attention(query, keys, keep):
    scores = scores_of(query, keys, keep)
    top = jnp.max(scores, axis=-1, keepdims=True)
    total = jnp.sum(jnp.exp(scores - top), axis=-1, keepdims=True)
    log_total = top + jnp.log(total)
    weights = jnp.exp(scores - log_total).astype(jnp.bfloat16)
    mixed = jnp.einsum(
        "ihtu,iud->ithd", weights, keys[..., HD:], preferred_element_type=jnp.float32
    )
    return (mixed.reshape(query.shape).astype(jnp.bfloat16), log_total)


def attention_back(query, keys, keep, log_total, grad_mixed):
    scores = scores_of(query, keys, keep)
    weights = jnp.exp(scores - log_total)
    heads_grad = grad_mixed.reshape(query.shape[0], query.shape[1], HEADS, HD)
    heads = query.reshape(heads_grad.shape)
    grad_weights = jnp.einsum(
        "ithd,iud->ihtu", heads_grad, keys[..., HD:], preferred_element_type=jnp.float32
    )
    inner = jnp.sum(weights * grad_weights, axis=-1, keepdims=True)
    grad_scores = (weights * (grad_weights - inner)).astype(jnp.bfloat16)
    scale = 1.0 / math.sqrt(HD)
    grad_query = (
        jnp.einsum(
            "ihtu,iud->ithd", grad_scores, keys[..., :HD], preferred_element_type=jnp.float32
        )
        * scale
    )
    grad_key = (
        jnp.einsum("ihtu,ithd->iud", grad_scores, heads, preferred_element_type=jnp.float32) * scale
    )
    grad_value = jnp.einsum(
        "ihtu,ithd->iud",
        weights.astype(jnp.bfloat16),
        heads_grad,
        preferred_element_type=jnp.float32,
    )
    return (grad_query.reshape(query.shape), jnp.concatenate([grad_key, grad_value], axis=-1))


def ffn_back(grad_rows, normed_rows, gate, up_part, hidden, gate_up, down):
    grad_hidden = project_back(grad_rows, down)
    _, pull = jax.vjp(geglu, gate, up_part)
    grad_gate, grad_up = pull(grad_hidden)
    grad_gate = grad_gate.astype(jnp.bfloat16)
    grad_up = grad_up.astype(jnp.bfloat16)
    gate_up_grad = jnp.stack(
        [outer_sum(normed_rows, grad_gate), outer_sum(normed_rows, grad_up)], axis=0
    )
    down_grad = outer_sum(hidden, grad_rows)
    grad_normed = project_back(grad_gate, gate_up[0]) + project_back(grad_up, gate_up[1])
    return (gate_up_grad, down_grad, grad_normed)


def on_device(
    prefix_in,
    action_in,
    prefix_len,
    action_count,
    loss_weight,
    prefix_gains,
    action_gains,
    prefix_qkv,
    prefix_out_proj,
    action_qkv,
    action_out_proj,
    prefix_gate_up,
    prefix_down,
    action_gate_up,
    action_down,
    prefix_cot,
    action_cot,
):
    width_q = HEADS * HD
    shard_rank = lax.axis_index("mp")
    shard_count = lax.axis_size("mp")
    items_here = prefix_in.shape[0]
    slab_rows = prefix_in.shape[1]
    action_rows = action_in.shape[1]
    whole_len = slab_rows * shard_count
    full_qkv_p, full_out_p, full_qkv_a, full_out_a, gains_full_p, gains_full_a = (
        lax.all_gather(prefix_qkv, ("dp", "mp"), axis=0, tiled=True),
        lax.all_gather(prefix_out_proj, ("dp", "mp"), axis=0, tiled=True),
        lax.all_gather(action_qkv, ("dp", "mp"), axis=0, tiled=True),
        lax.all_gather(action_out_proj, ("dp", "mp"), axis=0, tiled=True),
        lax.all_gather(prefix_gains, ("dp", "mp"), axis=0, tiled=True),
        lax.all_gather(action_gains, ("dp", "mp"), axis=0, tiled=True),
    )
    gate_up_p, down_p, gate_up_a, down_a = (
        lax.all_gather(prefix_gate_up, "dp", axis=1, tiled=True),
        lax.all_gather(prefix_down, "dp", axis=1, tiled=True),
        lax.all_gather(action_gate_up, "dp", axis=1, tiled=True),
        lax.all_gather(action_down, "dp", axis=1, tiled=True),
    )
    gain_attn_p = gains_full_p[:, 0].astype(jnp.float32)
    gain_ffn_p = gains_full_p[:, 1].astype(jnp.float32)
    gain_attn_a = gains_full_a[:, 0].astype(jnp.float32)
    gain_ffn_a = gains_full_a[:, 1].astype(jnp.float32)
    input_p = prefix_in.astype(jnp.float32)
    input_a = action_in.astype(jnp.float32)
    h_attn_p = normed(input_p, gain_attn_p).astype(jnp.bfloat16)
    h_attn_a = normed(input_a, gain_attn_a).astype(jnp.bfloat16)
    qkv_full_p = project(h_attn_p, full_qkv_p)
    qkv_full_a = project(h_attn_a, full_qkv_a)
    query_p = qkv_full_p[..., :width_q].astype(jnp.bfloat16)
    kv_prefix = qkv_full_p[..., width_q:].astype(jnp.bfloat16)
    query_a = qkv_full_a[..., :width_q].astype(jnp.bfloat16)
    kv_action = qkv_full_a[..., width_q:].astype(jnp.bfloat16)
    keys_all = lax.all_gather(kv_prefix, "mp", axis=1, tiled=True)
    keep_prefix = jnp.arange(whole_len, dtype=jnp.int32)[None, :] < prefix_len[:, None]
    keep_act_own = jnp.arange(action_rows, dtype=jnp.int32)[None, :] < action_count[:, None]
    keep_joined = jnp.concatenate([keep_prefix, keep_act_own], axis=1)
    keys_joined = jnp.concatenate([keys_all, kv_action], axis=1)
    mixed_p, log_total_p = attention(query_p, keys_all, keep_prefix)
    mixed_a, log_total_a = attention(query_a, keys_joined, keep_joined)
    mid_p = input_p + project(mixed_p, full_out_p)
    mid_a = input_a + project(mixed_a, full_out_a)
    h_ffn_p = normed(mid_p, gain_ffn_p).astype(jnp.bfloat16)
    h_ffn_all = lax.all_gather(h_ffn_p, "mp", axis=1, tiled=True)
    gate_p = project(h_ffn_all, gate_up_p[0])
    up_p = project(h_ffn_all, gate_up_p[1])
    hidden_p = geglu(gate_p, up_p).astype(jnp.bfloat16)
    ffn_p = lax.psum_scatter(
        project(hidden_p, down_p).astype(jnp.bfloat16), "mp", scatter_dimension=1, tiled=True
    ).astype(jnp.float32)
    h_ffn_a = normed(mid_a, gain_ffn_a).astype(jnp.bfloat16)
    gate_a = project(h_ffn_a, gate_up_a[0])
    up_a = project(h_ffn_a, gate_up_a[1])
    hidden_a = geglu(gate_a, up_a).astype(jnp.bfloat16)
    ffn_a = lax.psum(project(hidden_a, down_a).astype(jnp.bfloat16), "mp").astype(jnp.float32)
    out_p = mid_p + ffn_p
    out_a = mid_a + ffn_a
    weight = loss_weight.astype(jnp.float32)
    keep_own = lax.dynamic_slice_in_dim(keep_prefix, shard_rank * slab_rows, slab_rows, 1)
    grad_out_p = (
        prefix_cot.astype(jnp.float32)
        * (weight[:, None] * keep_own.astype(jnp.float32))[:, :, None]
    )
    grad_out_a = (
        action_cot.astype(jnp.float32)
        * (weight[:, None] * keep_act_own.astype(jnp.float32))[:, :, None]
    )
    share = jnp.arange(items_here * action_rows, dtype=jnp.int32) % shard_count == shard_rank
    share = share.reshape(items_here, action_rows)[:, :, None]
    back_gate_up_p, back_down_p, back_gate_up_a, back_down_a = (
        lax.all_gather(prefix_gate_up, "dp", axis=1, tiled=True),
        lax.all_gather(prefix_down, "dp", axis=1, tiled=True),
        lax.all_gather(action_gate_up, "dp", axis=1, tiled=True),
        lax.all_gather(action_down, "dp", axis=1, tiled=True),
    )
    grad_rows_p = lax.all_gather(grad_out_p.astype(jnp.bfloat16), "mp", axis=1, tiled=True)
    gate_up_grad_p, down_grad_p, grad_normed_p = ffn_back(
        grad_rows_p, h_ffn_all, gate_p, up_p, hidden_p, back_gate_up_p, back_down_p
    )
    grad_h_ffn_p = lax.psum_scatter(
        grad_normed_p.astype(jnp.bfloat16), "mp", scatter_dimension=1, tiled=True
    ).astype(jnp.float32)
    gate_up_grad_a, down_grad_a, grad_normed_a = ffn_back(
        grad_out_a.astype(jnp.bfloat16),
        h_ffn_a,
        gate_a,
        up_a,
        hidden_a,
        back_gate_up_a,
        back_down_a,
    )
    grad_h_ffn_a = lax.psum(grad_normed_a.astype(jnp.bfloat16), "mp").astype(jnp.float32)
    ffn_grads = (
        lax.psum_scatter(
            gate_up_grad_p.astype(jnp.bfloat16), "dp", scatter_dimension=1, tiled=True
        ).astype(jnp.float32),
        lax.psum_scatter(
            down_grad_p.astype(jnp.bfloat16), "dp", scatter_dimension=1, tiled=True
        ).astype(jnp.float32),
        lax.psum_scatter(
            gate_up_grad_a.astype(jnp.bfloat16), "dp", scatter_dimension=1, tiled=True
        ).astype(jnp.float32),
        lax.psum_scatter(
            down_grad_a.astype(jnp.bfloat16), "dp", scatter_dimension=1, tiled=True
        ).astype(jnp.float32),
    )
    _, pull_ffn_p = jax.vjp(normed, mid_p, gain_ffn_p)
    grad_from_p, gain_ffn_grad_p = pull_ffn_p(grad_h_ffn_p)
    grad_mid_p = grad_out_p + grad_from_p
    _, pull_ffn_a = jax.vjp(normed, mid_a, gain_ffn_a)
    grad_from_a, _ = pull_ffn_a(grad_h_ffn_a)
    _, gain_ffn_grad_a = pull_ffn_a(grad_h_ffn_a * share.astype(jnp.float32))
    grad_mid_a = grad_out_a + grad_from_a
    low_mid_p = grad_mid_p.astype(jnp.bfloat16)
    low_mid_a = grad_mid_a.astype(jnp.bfloat16)
    share_low = share.astype(jnp.bfloat16)
    out_proj_grad_p = outer_sum(mixed_p, low_mid_p)
    out_proj_grad_a = outer_sum(mixed_a * share_low, low_mid_a)
    grad_mixed_p = project_back(low_mid_p, full_out_p).astype(jnp.bfloat16)
    grad_mixed_a = project_back(low_mid_a, full_out_a).astype(jnp.bfloat16)
    keys_back = lax.all_gather(kv_prefix, "mp", axis=1, tiled=True)
    keys_joined_back = jnp.concatenate([keys_back, kv_action], axis=1)
    grad_query_p, grad_kv_terms = attention_back(
        query_p, keys_back, keep_prefix, log_total_p, grad_mixed_p
    )
    grad_query_a, grad_kv_joined = attention_back(
        query_a, keys_joined_back, keep_joined, log_total_a, grad_mixed_a
    )
    grad_kv_own = lax.psum_scatter(
        grad_kv_terms.astype(jnp.bfloat16), "mp", scatter_dimension=1, tiled=True
    ).astype(jnp.float32)
    grad_kv_own = grad_kv_own + lax.dynamic_slice_in_dim(
        grad_kv_joined[:, :whole_len], shard_rank * slab_rows, slab_rows, 1
    )
    grad_qkv_p = jnp.concatenate([grad_query_p, grad_kv_own], axis=-1).astype(jnp.bfloat16)
    grad_qkv_a = jnp.concatenate([grad_query_a, grad_kv_joined[:, whole_len:]], axis=-1).astype(
        jnp.bfloat16
    )
    qkv_grad_p = outer_sum(h_attn_p, grad_qkv_p)
    qkv_grad_a = outer_sum(h_attn_a * share_low, grad_qkv_a)
    grad_h_attn_p = project_back(grad_qkv_p, full_qkv_p)
    grad_h_attn_a = project_back(grad_qkv_a, full_qkv_a)
    _, pull_attn_p = jax.vjp(normed, input_p, gain_attn_p)
    grad_in_from_p, gain_attn_grad_p = pull_attn_p(grad_h_attn_p)
    _, pull_attn_a = jax.vjp(normed, input_a, gain_attn_a)
    grad_in_from_a, _ = pull_attn_a(grad_h_attn_a)
    _, gain_attn_grad_a = pull_attn_a(grad_h_attn_a * share.astype(jnp.float32))
    prefix_in_grad = grad_mid_p + grad_in_from_p
    action_in_grad = grad_mid_a + grad_in_from_a
    gains_grad_p = jnp.stack([gain_attn_grad_p, gain_ffn_grad_p], axis=1)
    gains_grad_a = jnp.stack([gain_attn_grad_a, gain_ffn_grad_a], axis=1)
    attn_sums = (
        lax.psum_scatter(qkv_grad_p, ("dp", "mp"), scatter_dimension=0, tiled=True),
        lax.psum_scatter(out_proj_grad_p, ("dp", "mp"), scatter_dimension=0, tiled=True),
        lax.psum_scatter(qkv_grad_a, ("dp", "mp"), scatter_dimension=0, tiled=True),
        lax.psum_scatter(out_proj_grad_a, ("dp", "mp"), scatter_dimension=0, tiled=True),
        lax.psum_scatter(gains_grad_p, ("dp", "mp"), scatter_dimension=0, tiled=True),
        lax.psum_scatter(gains_grad_a, ("dp", "mp"), scatter_dimension=0, tiled=True),
    )
    return (
        out_p.astype(jnp.bfloat16),
        out_a.astype(jnp.bfloat16),
        prefix_in_grad,
        action_in_grad,
        attn_sums[4],
        attn_sums[5],
        attn_sums[0],
        attn_sums[1],
        attn_sums[2],
        attn_sums[3],
        ffn_grads[0],
        ffn_grads[1],
        ffn_grads[2],
        ffn_grads[3],
    )


def solution(mesh):
    in_specs = (
        P("dp", "mp", None),
        P("dp", None, None),
        P("dp"),
        P("dp"),
        P("dp"),
        P(("dp", "mp"), None),
        P(("dp", "mp"), None),
        P(("dp", "mp"), None),
        P(("dp", "mp"), None),
        P(("dp", "mp"), None),
        P(("dp", "mp"), None),
        P(None, "dp", "mp"),
        P("mp", "dp"),
        P(None, "dp", "mp"),
        P("mp", "dp"),
        P("dp", "mp", None),
        P("dp", None, None),
    )
    out_specs = (
        P("dp", "mp", None),
        P("dp", None, None),
        P("dp", "mp", None),
        P("dp", None, None),
        P(("dp", "mp"), None),
        P(("dp", "mp"), None),
        P(("dp", "mp"), None),
        P(("dp", "mp"), None),
        P(("dp", "mp"), None),
        P(("dp", "mp"), None),
        P(None, "dp", "mp"),
        P("mp", "dp"),
        P(None, "dp", "mp"),
        P("mp", "dp"),
    )
    return jax.shard_map(
        on_device, mesh=mesh, in_specs=in_specs, out_specs=out_specs, check_vma=False
    )
```

profile of v0, /device:TPU:4, one launch (start us, length us, event | category | flops | bytes accessed | tf_op | source)
XLA Modules:
  0.0 2850.6 jit_solution(17849446859361098354)
XLA Ops:
  13.1 67.6 %all-gather = bf16[32,64,2]{1,2,0:T(2,128)(2,1)S(1)} all-gather(bf16[1,64,2]{1,2,0:T(2,128)(2,1)} %bitcast.394), channel_id=1, replica_groups=mesh['dp'=8,'mp'=4] {'dp','mp'}, dimensions={0}, use_global_device_ids=true | all-gather | bytes 8448 | tf_op jit(solution)/shard_map/all_gather | solution.py:128
  105.1 19.2 all_gather.46
  126.6 53.5 %all-gather.15.cloned.1.call-done = bf16[2048,2048]{1,0:T(8,128)(2,1)} async-done(((bf16[64,2048]{1,0:T(8,128)(2,1)}), bf16[2048,2048]{1,0:T(8,128)(2,1)}) %all-gather.15.cloned.1.call-update) | async-done | bytes 8388624 | tf_op jit(solution)/shard_map/all_gather | solution.py:125
  190.0 65.7 %all-gather.1 = bf16[32,32,2]{1,2,0:T(2,128)(2,1)S(1)} all-gather(bf16[1,32,2]{1,2,0:T(2,128)(2,1)S(1)} %bitcast.395), channel_id=1, replica_groups=mesh['dp'=8,'mp'=4] {'dp','mp'}, dimensions={0}, use_global_device_ids=true | all-gather | bytes 4224 | tf_op jit(solution)/shard_map/all_gather | solution.py:129
  262.5 48.4 %all-gather.25.cloned.1.call-done = bf16[2048,1024]{1,0:T(8,128)(2,1)} async-done(((bf16[64,1024]{1,0:T(8,128)(2,1)}), bf16[2048,1024]{1,0:T(8,128)(2,1)}) %all-gather.25.cloned.1.call-update) | async-done | bytes 4194320 | tf_op jit(solution)/shard_map/all_gather | solution.py:127
  314.2 33.6 %all-gather.27.cloned.1.call-done = bf16[2,1024,1024]{2,1,0:T(8,128)(2,1)} async-done(((bf16[2,128,1024]{2,1,0:T(8,128)(2,1)}), bf16[2,1024,1024]{2,1,0:T(8,128)(2,1)}) %all-gather.27.cloned.1.call-update) | async-done | bytes 4194320 | tf_op jit(solution)/shard_map/all_gather | solution.py:134
  351.9 25.7 all-gather.29.cloned.1.call-done
  385.5 40.5 %all-gather.17.cloned.1.call-done = bf16[1,512,2048]{2,1,0:T(8,128)(2,1)} async-done(((bf16[1,128,2048]{2,1,0:T(8,128)(2,1)}), bf16[1,512,2048]{2,1,0:T(8,128)(2,1)}) %all-gather.17.cloned.1.call-update) | async-done | bytes 2097168 | tf_op jit(solution)/shard_map/all_gather | solution.py:161
  426.0 160.3 %all-gather.19.cloned.1.call-done = bf16[2,2048,4096]{2,1,0:T(8,128)(2,1)} async-done(((bf16[2,256,4096]{2,1,0:T(8,128)(2,1)}), bf16[2,2048,4096]{2,1,0:T(8,128)(2,1)}) %all-gather.19.cloned.1.call-update) | async-done | bytes 33554448 | tf_op jit(solution)/shard_map/all_gather | solution.py:132
  635.6 92.4 %all-gather.21.cloned.1.call-done = bf16[4096,2048]{1,0:T(8,128)(2,1)} async-done(((bf16[4096,256]{1,0:T(8,128)(2,1)}), bf16[4096,2048]{1,0:T(8,128)(2,1)}) %all-gather.21.cloned.1.call-update) | async-done | bytes 16777232 | tf_op jit(solution)/shard_map/all_gather | solution.py:133
  728.0 22.6 multiply_convert_fusion
  806.0 20.5 reduce-scatter.24.cloned.1.call-done
  829.0 43.5 %reduce-scatter.22.cloned.1.call-done = bf16[1,128,2048]{2,1,0:T(8,128)(2,1)} async-done(((bf16[1,512,2048]{2,1,0:T(8,128)(2,1)}), bf16[1,128,2048]{2,1,0:T(8,128)(2,1)}) %reduce-scatter.22.cloned.1.call-update) | async-done | bytes 524304 | tf_op jit(solution)/shard_map/reduce_scatter | solution.py:165
  971.7 22.7 pad_maximum_fusion
  1028.8 20.6 reduce-scatter.44.cloned.1.call-done
  1050.7 40.2 %reduce-scatter.46.cloned.1.call-done = bf16[128,1024]{1,0:T(8,128)(2,1)} async-done(((bf16[1024,1024]{1,0:T(8,128)(2,1)}), bf16[128,1024]{1,0:T(8,128)(2,1)}) %reduce-scatter.46.cloned.1.call-update) | async-done | bytes 262160
  1092.9 53.6 %reduce-scatter.38.cloned.1.call-done = bf16[2,128,1024]{2,1,0:T(8,128)(2,1)} async-done(((bf16[2,1024,1024]{2,1,0:T(8,128)(2,1)}), bf16[2,128,1024]{2,1,0:T(8,128)(2,1)}) %reduce-scatter.38.cloned.1.call-update) | async-done | bytes 524304 | tf_op jit(solution)/shard_map/reduce_scatter | solution.py:217
  1149.9 133.6 %reduce-scatter.42.cloned.1.call-done = f32[64,2]{1,0:T(8,128)} async-done(((f32[2048,2]{1,0:T(8,128)}), f32[64,2]{1,0:T(8,128)}) %reduce-scatter.42.cloned.1.call-update) | async-done | bytes 528
  1284.9 115.9 %reduce-scatter.36.cloned.1.call-done = bf16[4096,256]{1,0:T(8,128)(2,1)} async-done(((bf16[4096,2048]{1,0:T(8,128)(2,1)}), bf16[4096,256]{1,0:T(8,128)(2,1)}) %reduce-scatter.36.cloned.1.call-update) | async-done | bytes 2097168 | tf_op jit(solution)/shard_map/reduce_scatter | solution.py:214
  1404.7 205.2 %reduce-scatter.34.cloned.1.call-done = bf16[2,256,4096]{2,1,0:T(8,128)(2,1)} async-done(((bf16[2,2048,4096]{2,1,0:T(8,128)(2,1)}), bf16[2,256,4096]{2,1,0:T(8,128)(2,1)}) %reduce-scatter.34.cloned.1.call-update) | async-done | bytes 4194320 | tf_op jit(solution)/shard_map/reduce_scatter | solution.py:211
  1616.5 181.2 %reduce-scatter.32.cloned.1.call-done = f32[64,1024]{1,0:T(8,128)} async-done(((f32[2048,1024]{1,0:T(8,128)}), f32[64,1024]{1,0:T(8,128)}) %reduce-scatter.32.cloned.1.call-update) | async-done | bytes 262160 | tf_op jit(solution)/shard_map/reduce_scatter | solution.py:273
  1797.7 229.8 %reduce-scatter.30.cloned.1.call-done = f32[32,2560]{1,0:T(8,128)} async-done(((f32[1024,2560]{1,0:T(8,128)}), f32[32,2560]{1,0:T(8,128)}) %reduce-scatter.30.cloned.1.call-update) | async-done | bytes 327696 | tf_op jit(solution)/shard_map/reduce_scatter | solution.py:272
  2027.6 364.5 %reduce-scatter.28.cloned.1.call-done = f32[64,2048]{1,0:T(8,128)} async-done(((f32[2048,2048]{1,0:T(8,128)}), f32[64,2048]{1,0:T(8,128)}) %reduce-scatter.28.cloned.1.call-update) | async-done | bytes 524304 | tf_op jit(solution)/shard_map/reduce_scatter | solution.py:271
  2392.1 451.3 %reduce-scatter.26.cloned.1.call-done = f32[64,2560]{1,0:T(8,128)} async-done(((f32[2048,2560]{1,0:T(8,128)}), f32[64,2560]{1,0:T(8,128)}) %reduce-scatter.26.cloned.1.call-update) | async-done | bytes 655376 | tf_op jit(solution)/shard_map/reduce_scatter | solution.py:270
  (333 shorter events, 320.6 us)
Async XLA Ops:
  7.2 91.8 %all-gather.13.cloned.1.call-start = ((), (), s32[]{:S(2)}) async-start(), calls=%async_computation.13 | async-start | bytes 10813440 | tf_op jit(solution)/shard_map/all_gather | solution.py:124
  7.9 172.2 %all-gather.15.cloned.1.call-start = ((), (), s32[]{:S(2)}) async-start(), calls=%async_computation.14 | async-start | bytes 8650752 | tf_op jit(solution)/shard_map/all_gather | solution.py:125
  8.7 248.1 %all-gather.23.cloned.1.call-start = ((), (), s32[]{:S(2)}) async-start(), calls=%async_computation.19 | async-start | bytes 5406720 | tf_op jit(solution)/shard_map/all_gather | solution.py:126
  9.4 301.5 %all-gather.25.cloned.1.call-start = ((), (), s32[]{:S(2)}) async-start(), calls=%async_computation.20 | async-start | bytes 4325376 | tf_op jit(solution)/shard_map/all_gather | solution.py:127
  10.0 337.8 %all-gather.27.cloned.1.call-start = ((), (), s32[]{:S(2)}) async-start(), calls=%async_computation.21 | async-start | bytes 4718592 | tf_op jit(solution)/shard_map/all_gather | solution.py:134
  10.6 367.0 %all-gather.29.cloned.1.call-start = ((), (), s32[]{:S(2)}) async-start(), calls=%async_computation.22 | async-start | bytes 2359296 | tf_op jit(solution)/shard_map/all_gather | solution.py:135
  11.1 414.9 %all-gather.17.cloned.1.call-start = ((), (), s32[]{:S(2)}) async-start(), calls=%async_computation.15 | async-start | bytes 2621440 | tf_op jit(solution)/shard_map/all_gather | solution.py:161
  186.9 399.4 %all-gather.19.cloned.1.call-start = ((), (), s32[]{:S(2)}) async-start(), calls=%async_computation.16 | async-start | bytes 37748736 | tf_op jit(solution)/shard_map/all_gather | solution.py:132
  187.6 448.0 %all-gather.31.cloned.1.call-start = ((), (), s32[]{:S(2)}) async-start(), calls=%async_computation.23 | async-start | bytes 2621440 | tf_op jit(solution)/shard_map/all_gather | solution.py:193
  189.3 538.7 %all-gather.21.cloned.1.call-start = ((), (), s32[]{:S(2)}) async-start(), calls=%async_computation.17 | async-start | bytes 18874368 | tf_op jit(solution)/shard_map/all_gather | solution.py:133
  190.0 606.4 %all-reduce.3.cloned.1.call-start = ((), (), s32[]{:S(2)}) async-start(), calls=%async_computation.36 | async-start | bytes 458752 | tf_op jit(solution)/shard_map/psum | solution.py:172
  385.3 441.2 %reduce-scatter.24.cloned.1.call-start = ((), (), s32[]{:S(2)}) async-start(), calls=%async_computation.24 | async-start | bytes 2621440 | tf_op jit(solution)/shard_map/reduce_scatter | solution.py:197
  781.3 91.3 %reduce-scatter.22.cloned.1.call-start = ((), (), s32[]{:S(2)}) async-start(), calls=%async_computation.18 | async-start | bytes 2621440 | tf_op jit(solution)/shard_map/reduce_scatter | solution.py:165
  795.9 120.6 %reduce-scatter.40.cloned.1.call-start = ((), (), s32[]{:S(2)}) async-start(), calls=%async_computation.32 | async-start | bytes 655360
  894.1 155.3 %reduce-scatter.44.cloned.1.call-start = ((), (), s32[]{:S(2)}) async-start(), calls=%async_computation.34 | async-start | bytes 540672
  903.8 187.1 %reduce-scatter.46.cloned.1.call-start = ((), (), s32[]{:S(2)}) async-start(), calls=%async_computation.35 | async-start | bytes 2359296
  908.0 238.5 %reduce-scatter.38.cloned.1.call-start = ((), (), s32[]{:S(2)}) async-start(), calls=%async_computation.31 | async-start | bytes 4718592 | tf_op jit(solution)/shard_map/reduce_scatter | solution.py:217
  912.2 371.3 %reduce-scatter.42.cloned.1.call-start = ((), (), s32[]{:S(2)}) async-start(), calls=%async_computation.33 | async-start | bytes 1081344
  928.6 472.2 %reduce-scatter.36.cloned.1.call-start = ((), (), s32[]{:S(2)}) async-start(), calls=%async_computation.30 | async-start | bytes 18874368 | tf_op jit(solution)/shard_map/reduce_scatter | solution.py:214
  943.7 666.1 %reduce-scatter.34.cloned.1.call-start = ((), (), s32[]{:S(2)}) async-start(), calls=%async_computation.29 | async-start | bytes 37748736 | tf_op jit(solution)/shard_map/reduce_scatter | solution.py:211
  994.4 803.3 %reduce-scatter.32.cloned.1.call-start = ((), (), s32[]{:S(2)}) async-start(), calls=%async_computation.28 | async-start | bytes 8650752 | tf_op jit(solution)/shard_map/reduce_scatter | solution.py:273
  1000.1 1027.5 %reduce-scatter.30.cloned.1.call-start = ((), (), s32[]{:S(2)}) async-start(), calls=%async_computation.27 | async-start | bytes 10813440 | tf_op jit(solution)/shard_map/reduce_scatter | solution.py:272
  1006.7 1385.4 %reduce-scatter.28.cloned.1.call-start = ((), (), s32[]{:S(2)}) async-start(), calls=%async_computation.26 | async-start | bytes 17301504 | tf_op jit(solution)/shard_map/reduce_scatter | solution.py:271
  1016.2 1827.2 %reduce-scatter.26.cloned.1.call-start = ((), (), s32[]{:S(2)}) async-start(), calls=%async_computation.25 | async-start | bytes 21626880 | tf_op jit(solution)/shard_map/reduce_scatter | solution.py:270
  (80 other events, 3314.7 us)
Sparse Core Ops, SparseCore 0:
  10.8 88.0 all-gather.12
  101.9 78.1 all-gather.14
  183.0 63.9 all-gather.22
  249.9 60.9 all-gather.24
  312.6 35.1 all-gather.26
  349.5 28.0 all-gather.28
  379.7 46.2 all-gather.16
  427.9 158.3 all-gather.18
  588.5 47.0 all-gather.30
  637.3 90.6 all-gather.20
  731.0 36.3 all-reduce.2
  781.4 45.0 reduce-scatter.23
  829.3 43.1 reduce-scatter.21
  894.2 20.9 reduce-scatter.39
  917.9 131.4 reduce-scatter.43
  1052.5 38.3 reduce-scatter.45
  1095.1 51.3 reduce-scatter.37
  1148.6 134.8 reduce-scatter.41
  1287.5 113.2 reduce-scatter.35
  1404.6 205.2 reduce-scatter.33
  1612.7 184.9 reduce-scatter.31
  1800.6 226.8 reduce-scatter.29
  2030.4 361.6 reduce-scatter.27
  2394.8 448.4 reduce-scatter.25
where the time goes:
time: 2860 us; the launch traced here: 2850 us
  waiting for transfers between devices  2360 us (83%)
  matrix products  238 us (8%)
  blocking collectives  152 us (5%)
  other arithmetic  54.6 us (2%)
  local copies, waits for them, and re-layouts  30.6 us (1%)
    reduce_scatter x1, waiting for transfers between devices, on_device(): lax.psum_scatter(qkv_grad_p, ('dp', 'mp'), scatter_dimension=0, tiled=True)  451 us
    reduce_scatter x1, waiting for transfers between devices, on_device(): lax.psum_scatter(out_proj_grad_p, ('dp', 'mp'), scatter_dimension=0, tile...  365 us
    reduce_scatter x1, waiting for transfers between devices, on_device(): lax.psum_scatter(qkv_grad_a, ('dp', 'mp'), scatter_dimension=0, tiled=True)  230 us
    reduce_scatter x1, waiting for transfers between devices, on_device(): lax.psum_scatter(gate_up_grad_p.astype(jnp.bfloat16), 'dp', scatter_dimen...  205 us
    unnamed x28, waiting for transfers between devices  200 us
    reduce_scatter x1, waiting for transfers between devices, on_device(): lax.psum_scatter(out_proj_grad_a, ('dp', 'mp'), scatter_dimension=0, tile...  181 us
    all_gather x1, waiting for transfers between devices, on_device(): lax.all_gather(prefix_gate_up, 'dp', axis=1, tiled=True)  160 us
    reduce_scatter x1, waiting for transfers between devices, on_device(): lax.psum_scatter(down_grad_p.astype(jnp.bfloat16), 'dp', scatter_dimensio...  116 us
  transfers between devices with their start and end apart: 24, of which 21 were waited for; matrix products, arithmetic and copies ran while one was open for 10% of the time, Pallas kernels for 0%

commit v1 on v0

v1 whole, which is shorter than its diff:
```python
import math

import jax
import jax.numpy as jnp
from jax import lax
from jax.sharding import PartitionSpec as P

HEADS = 8
HD = 256
WIDTH_Q = HEADS * HD
INNER = 4
BF = jnp.bfloat16
F32 = jnp.float32

EPS = 1e-06


def dot(left, right, contract):
    return lax.dot_general(left, right, (contract, ((), ())), preferred_element_type=F32)


def mm(left, right):
    return dot(left, right, ((1,), (0,)))


def mm_nt(left, right):
    return dot(left, right, ((1,), (1,)))


def mm_tn(left, right):
    return dot(left, right, ((0,), (0,)))


def normed(values, gain):
    scale = lax.rsqrt(jnp.mean(values * values, axis=-1, keepdims=True) + EPS)
    return values * scale * gain


def geglu(gate, up_part):
    return jax.nn.gelu(gate, approximate=True) * up_part


def swap(value, mask):
    size = lax.axis_size("dp")
    return lax.ppermute(value, "dp", [(i, i ^ mask) for i in range(size)])


def shift(value):
    size = lax.axis_size("mp")
    return lax.ppermute(value, "mp", [(i, (i + 1) % size) for i in range(size)])


def ring_gather(value):
    blocks = [value]
    for _ in range(lax.axis_size("mp") - 1):
        blocks.append(shift(blocks[-1]))
    return blocks


def ring_scatter(blocks):
    total = blocks[1] if len(blocks) > 1 else blocks[0]
    for block in blocks[2:]:
        total = shift(total.astype(BF)).astype(F32) + block
    if len(blocks) > 1:
        total = shift(total.astype(BF)).astype(F32) + blocks[0]
    return total


def block_order(masks):
    order = [0]
    for mask in masks:
        order = order + [j ^ mask for j in order]
    return order


def xor_blocks(value, index, count, axis, order=None):
    size = value.shape[axis] // count
    parts = [lax.slice_in_dim(value, j * size, (j + 1) * size, axis=axis) for j in range(count)]
    bit = 1
    while bit < count:
        on = (index & bit) != 0
        parts = [jnp.where(on, parts[j ^ bit], parts[j]) for j in range(count)]
        bit *= 2
    order = order if order is not None else range(count)
    return jnp.concatenate([parts[j] for j in order], axis=axis)


def unxor_blocks(value, index, count, axis, order):
    size = value.shape[axis] // count
    place = {j: p for p, j in enumerate(order)}
    parts = [
        lax.slice_in_dim(value, place[j] * size, (place[j] + 1) * size, axis=axis)
        for j in range(count)
    ]
    bit = 1
    while bit < count:
        on = (index & bit) != 0
        parts = [jnp.where(on, parts[j ^ bit], parts[j]) for j in range(count)]
        bit *= 2
    return jnp.concatenate(parts, axis=axis)


def dp_gather(value, masks):
    for mask in masks:
        value = jnp.concatenate([value, swap(value, mask)], axis=0)
    return value


def dp_scatter(value, masks):
    for mask in reversed(masks):
        half = value.shape[0] // 2
        value = value[:half] + swap(value[half:].astype(BF), mask).astype(F32)
    return value


def inner_exchange(value):
    size = lax.axis_size("dp")
    groups = [list(range(g, g + INNER)) for g in range(0, size, INNER)]
    return lax.all_to_all(value, "dp", 0, 0, axis_index_groups=groups, tiled=True)


def gather_tokens(rows):
    half = rows.shape[1] // 2
    first = jnp.stack(ring_gather(rows[:, :half]))
    first = jnp.stack([first, swap(first, 2)])
    second = jnp.stack([rows[:, half:], swap(rows[:, half:], 2)])
    second = jnp.stack(ring_gather(second), axis=1)
    out = []
    for part in (first, second):
        part = jnp.stack([part, swap(part, 1)])
        out.append(part.reshape(-1, half))
    return out


def scatter_tokens(first, second, rows):
    shard_count = lax.axis_size("mp")
    half = first.shape[1]
    parts = []
    for part in (first, second):
        part = part.reshape(2, 2, shard_count, rows, half)
        parts.append(part[0] + swap(part[1].astype(BF), 1).astype(F32))
    first = parts[0][0] + swap(parts[0][1].astype(BF), 2).astype(F32)
    first = ring_scatter([first[s] for s in range(shard_count)])
    second = ring_scatter([parts[1][:, s] for s in range(shard_count)])
    second = second[0] + swap(second[1].astype(BF), 2).astype(F32)
    return jnp.concatenate([first, second], axis=-1)


def spread(value, axes):
    size = math.prod(lax.axis_size(a) for a in axes)
    return lax.all_to_all(
        jnp.broadcast_to(value[None], (size,) + value.shape), axes, 0, 0, tiled=True
    )


def sum_mp(value):
    return jnp.sum(spread(value.astype(BF), ("mp",)).astype(F32), axis=0)


def scores_of(query, keys, keep):
    raw = jnp.einsum("thd,ud->htu", query, keys[:, :HD], preferred_element_type=F32)
    return jnp.where(keep[None, None, :], raw * (1.0 / math.sqrt(HD)), -1e30)


def attention(query, keys, keep):
    heads = query.reshape(query.shape[0], -1, HD)
    scores = scores_of(heads, keys, keep)
    top = jnp.max(scores, axis=-1, keepdims=True)
    weights = jnp.exp(scores - top)
    probs = weights / jnp.sum(weights, axis=-1, keepdims=True)
    mixed = jnp.einsum("htu,ud->thd", probs.astype(BF), keys[:, HD:], preferred_element_type=F32)
    return (mixed.reshape(query.shape).astype(BF), probs)


def attention_back(query, keys, probs, grad_mixed):
    heads = query.reshape(query.shape[0], -1, HD)
    heads_grad = grad_mixed.reshape(heads.shape)
    grad_probs = jnp.einsum("thd,ud->htu", heads_grad, keys[:, HD:], preferred_element_type=F32)
    inner = jnp.sum(probs * grad_probs, axis=-1, keepdims=True)
    grad_scores = (probs * (grad_probs - inner)).astype(BF)
    scale = 1.0 / math.sqrt(HD)
    grad_query = (
        jnp.einsum("htu,ud->thd", grad_scores, keys[:, :HD], preferred_element_type=F32) * scale
    )
    grad_key = jnp.einsum("htu,thd->ud", grad_scores, heads, preferred_element_type=F32) * scale
    grad_value = jnp.einsum("htu,thd->ud", probs.astype(BF), heads_grad, preferred_element_type=F32)
    return (grad_query.reshape(query.shape), jnp.concatenate([grad_key, grad_value], axis=-1))


def on_device(
    prefix_in,
    action_in,
    prefix_len,
    action_count,
    loss_weight,
    prefix_gains,
    action_gains,
    prefix_qkv,
    prefix_out_proj,
    action_qkv,
    action_out_proj,
    prefix_gate_up,
    prefix_down,
    action_gate_up,
    action_down,
    prefix_cot,
    action_cot,
):
    dp = lax.axis_index("dp")
    z = lax.axis_index("mp")
    dp_count = lax.axis_size("dp")
    shard_count = lax.axis_size("mp")
    outer = dp_count // INNER
    outer_index = dp // INNER
    slab = prefix_in.shape[1]
    width_p = prefix_in.shape[2]
    width_a = action_in.shape[2]
    action_rows = action_in.shape[1]
    whole_len = slab * shard_count
    query_here = WIDTH_Q // shard_count
    outer_masks = []
    mask = INNER
    while mask < dp_count:
        outer_masks.append(mask)
        mask *= 2
    masks_p = [2] + outer_masks + [1]
    masks_a = outer_masks + [2] + [1]
    order_p = block_order(masks_p)
    order_a = block_order(masks_a)
    everywhere = ("dp", "mp")

    rows_gp = prefix_gains.shape[0]
    rows_ga = action_gains.shape[0]
    gains_own = jnp.concatenate([prefix_gains.T.reshape(-1), action_gains.T.reshape(-1)])
    gains_all = spread(gains_own, everywhere).astype(F32)
    gains_p = gains_all[:, : 2 * rows_gp].reshape(-1, 2, rows_gp)
    gains_a = gains_all[:, 2 * rows_gp :].reshape(-1, 2, rows_ga)
    gain_attn_p = gains_p[:, 0].reshape(-1)
    gain_ffn_p = gains_p[:, 1].reshape(-1)
    gain_attn_a = gains_a[:, 0].reshape(-1)
    gain_ffn_a = gains_a[:, 1].reshape(-1)

    def heads_of(weights):
        rows = weights.shape[0]
        query = weights[:, :WIDTH_Q].reshape(rows, shard_count, query_here).transpose(1, 0, 2)
        both = jnp.broadcast_to(weights[None, :, WIDTH_Q:], (shard_count, rows, 2 * HD))
        own = lax.all_to_all(jnp.concatenate([query, both], axis=-1), "mp", 0, 0, tiled=True)
        return own.reshape(shard_count * rows, query_here + 2 * HD)

    total = dp_count * shard_count
    to_heads = [(j, (j % dp_count) * shard_count + j // dp_count) for j in range(total)]
    from_heads = [(b, a) for a, b in to_heads]
    qkv_p = dp_gather(heads_of(prefix_qkv), masks_p)
    qkv_a = dp_gather(heads_of(action_qkv), masks_a)
    out_own = jnp.concatenate([prefix_out_proj, action_out_proj], axis=1)
    out_own = lax.ppermute(out_own, everywhere, to_heads)
    out_both = unxor_blocks(dp_gather(out_own, masks_a), dp, dp_count, 0, order_a)
    out_p = out_both[:, :width_p]
    out_a = out_both[:, width_p:]

    def hidden_of(weights):
        rows, hidden = weights.shape
        cut = weights.reshape(rows, INNER, hidden // INNER).transpose(1, 0, 2)
        own = inner_exchange(cut).reshape(INNER * rows, hidden // INNER)
        for mask in outer_masks[:-1]:
            own = jnp.concatenate([own, swap(own, mask)], axis=0)
        return (own, swap(own, outer_masks[-1]))

    gate_w = hidden_of(prefix_gate_up[0])
    up_w = hidden_of(prefix_gate_up[1])
    down_w = hidden_of(prefix_down.T)

    def hidden_back(first, second):
        value = first + swap(second.astype(BF), outer_masks[-1]).astype(F32)
        for mask in reversed(outer_masks[:-1]):
            half = value.shape[0] // 2
            value = value[:half] + swap(value[half:].astype(BF), mask).astype(F32)
        rows = value.shape[0] // INNER
        value = inner_exchange(value.astype(BF).reshape(INNER, rows, value.shape[1]))
        return value.transpose(1, 0, 2).reshape(rows, -1).astype(F32)

    def hidden_of_a(weights):
        rows, hidden = weights.shape
        cut = weights.reshape(rows, dp_count, hidden // dp_count).transpose(1, 0, 2)
        own = lax.all_to_all(cut, "dp", 0, 0, tiled=True)
        return own.reshape(dp_count * rows, hidden // dp_count)

    def hidden_back_a(value):
        rows = value.shape[0] // dp_count
        value = value.astype(BF).reshape(dp_count, rows, value.shape[1])
        value = lax.all_to_all(value, "dp", 0, 0, tiled=True)
        return value.transpose(1, 0, 2).reshape(rows, -1).astype(F32)

    gate_wa = hidden_of_a(action_gate_up[0])
    up_wa = hidden_of_a(action_gate_up[1])
    down_wa = hidden_of_a(action_down.T)

    position = jnp.arange(whole_len, dtype=jnp.int32)
    ring_index = (z - position // slab + shard_count) % shard_count
    keep_prefix = ring_index * slab + position % slab < prefix_len[0]
    keep_action = jnp.arange(action_rows, dtype=jnp.int32) < action_count[0]
    keep_joined = jnp.concatenate([keep_prefix, keep_action])
    weight = loss_weight[0].astype(F32)
    keep_own = keep_prefix[:slab]
    grad_out_p = prefix_cot[0].astype(F32) * (weight * keep_own.astype(F32))[:, None]
    grad_out_a = action_cot[0].astype(F32) * (weight * keep_action.astype(F32))[:, None]

    x_p = prefix_in[0]
    x_a = action_in[0]
    input_p = x_p.astype(F32)
    input_a = x_a.astype(F32)
    x_all = jnp.concatenate(ring_gather(xor_blocks(x_p, dp, dp_count, 1, order_p)), axis=0)
    h_attn_p = normed(
        x_all.astype(F32), xor_blocks(gain_attn_p, dp, dp_count, 0, order_p)
    ).astype(BF)
    h_attn_a = normed(
        xor_blocks(input_a, dp, dp_count, 1, order_a),
        xor_blocks(gain_attn_a, dp, dp_count, 0, order_a),
    ).astype(BF)
    all_p = mm(h_attn_p, qkv_p).astype(BF)
    all_a = mm(h_attn_a, qkv_a).astype(BF)
    query_p, kv_p = all_p[:, :query_here], all_p[:, query_here:]
    query_a, kv_a = all_a[:, :query_here], all_a[:, query_here:]
    kv_joined = jnp.concatenate([kv_p, kv_a], axis=0)
    mixed_p, probs_p = attention(query_p, kv_p, keep_prefix)
    mixed_a, probs_a = attention(query_a, kv_joined, keep_joined)
    terms = mm(mixed_p, out_p)
    mid_p = input_p + ring_scatter([terms[s * slab : (s + 1) * slab] for s in range(shard_count)])
    mid_a = input_a + sum_mp(mm(mixed_a, out_a))

    h_ffn_p = normed(mid_p, gain_ffn_p).astype(BF)
    h0, h1 = gather_tokens(xor_blocks(h_ffn_p, outer_index, outer, 1))
    g0, g1 = gather_tokens(xor_blocks(grad_out_p.astype(BF), outer_index, outer, 1))
    gate = mm(h0, gate_w[0]) + mm(h1, gate_w[1])
    up_part = mm(h0, up_w[0]) + mm(h1, up_w[1])
    hidden, pull = jax.vjp(geglu, gate, up_part)
    hidden = hidden.astype(BF)
    d_gate, d_up = pull(mm(g0, down_w[0]) + mm(g1, down_w[1]))
    d_gate = d_gate.astype(BF)
    d_up = d_up.astype(BF)
    dh_terms = [mm_nt(d_gate, gate_w[i]) + mm_nt(d_up, up_w[i]) for i in range(2)]
    dh_p = xor_blocks(scatter_tokens(*dh_terms, slab), outer_index, outer, 1)
    out_terms = [mm_nt(hidden, down_w[i]) for i in range(2)]
    ffn_p = xor_blocks(scatter_tokens(*out_terms, slab), outer_index, outer, 1)
    prefix_out = (mid_p + ffn_p).astype(BF)
    gate_grad_p = hidden_back(mm_tn(h0, d_gate), mm_tn(h1, d_gate))
    up_grad_p = hidden_back(mm_tn(h0, d_up), mm_tn(h1, d_up))
    down_grad_p = hidden_back(mm_tn(g0, hidden), mm_tn(g1, hidden)).T

    h_ffn_a = normed(mid_a, gain_ffn_a).astype(BF)
    ha = spread(h_ffn_a, ("dp",)).reshape(-1, width_a)
    ga = spread(grad_out_a.astype(BF), ("dp",)).reshape(-1, width_a)
    hidden_a, pull_a = jax.vjp(geglu, mm(ha, gate_wa), mm(ha, up_wa))
    hidden_a = hidden_a.astype(BF)
    d_gate_a, d_up_a = pull_a(mm(ga, down_wa))
    d_gate_a = d_gate_a.astype(BF)
    d_up_a = d_up_a.astype(BF)
    terms_a = jnp.stack(
        [mm_nt(hidden_a, down_wa), mm_nt(d_gate_a, gate_wa) + mm_nt(d_up_a, up_wa)]
    )
    terms_a = terms_a.reshape(2, dp_count, action_rows, width_a).transpose(1, 0, 2, 3)
    terms_a = lax.all_to_all(terms_a.astype(BF), "dp", 0, 0, tiled=True)
    sums_a = sum_mp(jnp.sum(terms_a.astype(F32), axis=0))
    action_out = (mid_a + sums_a[0]).astype(BF)
    dh_a = sums_a[1]
    gate_grad_a = hidden_back_a(mm_tn(ha, d_gate_a))
    up_grad_a = hidden_back_a(mm_tn(ha, d_up_a))
    down_grad_a = hidden_back_a(mm_tn(ga, hidden_a)).T

    _, pull_ffn_p = jax.vjp(normed, mid_p, gain_ffn_p)
    from_ffn_p, gain_ffn_grad_p = pull_ffn_p(dh_p)
    d_mid_p = grad_out_p + from_ffn_p
    _, pull_ffn_a = jax.vjp(normed, mid_a, gain_ffn_a)
    from_ffn_a, gain_ffn_grad_a = pull_ffn_a(dh_a)
    d_mid_a = grad_out_a + from_ffn_a

    g_mid_p = jnp.concatenate(ring_gather(d_mid_p.astype(BF)), axis=0)
    g_mid_a = d_mid_a.astype(BF)
    out_grad = jnp.concatenate([mm_tn(mixed_p, g_mid_p), mm_tn(mixed_a, g_mid_a)], axis=1)
    out_grad = dp_scatter(xor_blocks(out_grad, dp, dp_count, 0, order_a), masks_a)
    out_grad = lax.ppermute(out_grad.astype(BF), everywhere, from_heads).astype(F32)
    d_mixed_p = mm_nt(g_mid_p, out_p).astype(BF)
    d_mixed_a = mm_nt(g_mid_a, out_a).astype(BF)
    d_query_p, d_kv_p = attention_back(query_p, kv_p, probs_p, d_mixed_p)
    d_query_a, d_kv_joined = attention_back(query_a, kv_joined, probs_a, d_mixed_a)
    d_kv_p = d_kv_p + d_kv_joined[:whole_len]
    d_all_p = jnp.concatenate([d_query_p, d_kv_p], axis=1).astype(BF)
    d_all_a = jnp.concatenate([d_query_a, d_kv_joined[whole_len:]], axis=1).astype(BF)

    def heads_back(value, masks):
        value = dp_scatter(value, masks).astype(BF)
        rows = value.shape[0] // shard_count
        value = value.reshape(shard_count, rows, value.shape[1])
        value = lax.all_to_all(value, "mp", 0, 0, tiled=True).astype(F32)
        query = value[:, :, :query_here].transpose(1, 0, 2).reshape(rows, WIDTH_Q)
        return jnp.concatenate([query, jnp.sum(value[:, :, query_here:], axis=0)], axis=1)

    qkv_grad_p = heads_back(mm_tn(h_attn_p, d_all_p), masks_p)
    qkv_grad_a = heads_back(mm_tn(h_attn_a, d_all_a), masks_a)
    terms = mm_nt(d_all_p, qkv_p)
    dh_attn_p = ring_scatter([terms[s * slab : (s + 1) * slab] for s in range(shard_count)])
    dh_attn_p = unxor_blocks(dh_attn_p, dp, dp_count, 1, order_p)
    dh_attn_a = unxor_blocks(sum_mp(mm_nt(d_all_a, qkv_a)), dp, dp_count, 1, order_a)
    _, pull_attn_p = jax.vjp(normed, input_p, gain_attn_p)
    from_attn_p, gain_attn_grad_p = pull_attn_p(dh_attn_p)
    _, pull_attn_a = jax.vjp(normed, input_a, gain_attn_a)
    from_attn_a, gain_attn_grad_a = pull_attn_a(dh_attn_a)

    once = (z == 0).astype(F32)
    gains_terms = jnp.concatenate(
        [
            jnp.stack([gain_attn_grad_p, gain_ffn_grad_p]).reshape(2, total, rows_gp),
            jnp.stack([gain_attn_grad_a, gain_ffn_grad_a]).reshape(2, total, rows_ga) * once,
        ],
        axis=2,
    ).transpose(1, 0, 2)
    gains_grad = jnp.sum(lax.all_to_all(gains_terms, everywhere, 0, 0, tiled=True), axis=0)
    return (
        prefix_out[None],
        action_out[None],
        (d_mid_p + from_attn_p)[None],
        (d_mid_a + from_attn_a)[None],
        gains_grad[:, :rows_gp].T,
        gains_grad[:, rows_gp:].T,
        qkv_grad_p,
        out_grad[:, :width_p],
        qkv_grad_a,
        out_grad[:, width_p:],
        jnp.stack([gate_grad_p, up_grad_p]),
        down_grad_p,
        jnp.stack([gate_grad_a, up_grad_a]),
        down_grad_a,
    )


def solution(mesh):
    rows = P(("dp", "mp"), None)
    tokens_p = P("dp", "mp", None)
    tokens_a = P("dp", None, None)
    gate_up = P(None, "dp", "mp")
    down = P("mp", "dp")
    per_item = P("dp")
    in_specs = (
        (tokens_p, tokens_a)
        + (per_item,) * 3
        + (rows,) * 6
        + (gate_up, down, gate_up, down)
        + (tokens_p, tokens_a)
    )
    out_specs = (
        (tokens_p, tokens_a, tokens_p, tokens_a) + (rows,) * 6 + (gate_up, down, gate_up, down)
    )
    return jax.shard_map(
        on_device, mesh=mesh, in_specs=in_specs, out_specs=out_specs, check_vma=False
    )
```

time: 2860 us -> 1150 us (0.40)
  waiting for transfers between devices: 2360 us -> 431 us
  starting transfers between devices: 2.18 us -> 174 us
  blocking collectives: 152 us -> 0 us
  local copies, waits for them, and re-layouts: 30.6 us -> 155 us
  other arithmetic: 54.6 us -> 162 us
    reduce_scatter x9 -> x0, waiting for transfers between devices: 1670 us -> none  [the longest x1 451 us: on_device(): lax.psum_scatter(qkv_grad_p, ('dp', 'mp'), scatter_dimension=0, tiled=True)]
    all_gather x10 -> x0, waiting for transfers between devices: 490 us -> none  [the longest x1 160 us: on_device(): lax.all_gather(prefix_gate_up, 'dp', axis=1, tiled=True)]
    ppermute x0 -> x78, waiting for transfers between devices: none -> 280 us  [the longest x40 160 us: swap(): return lax.ppermute(value, 'dp', [(i, i ^ mask) for i in range(size)])]
    unnamed x28 -> x0, waiting for transfers between devices: 200 us -> none
    all_gather x3 -> x0, blocking collectives: 152 us -> none  [the longest x1 67.6 us: on_device(): lax.all_gather(prefix_gains, ('dp', 'mp'), axis=0, tiled=True)]
    all_to_all x0 -> x24, waiting for transfers between devices: none -> 151 us  [the longest x6 80.3 us: spread(): lax.all_to_all(jnp.broadcast_to(value[None], (size,) + value.shape), axes...]
    all_to_all x0 -> x24, starting transfers between devices: none -> 107 us  [the longest x6 31.3 us: spread(): lax.all_to_all(jnp.broadcast_to(value[None], (size,) + value.shape), axes...]
    ppermute x0 -> x78, starting transfers between devices: none -> 67.6 us  [the longest x40 32.1 us: swap(): return lax.ppermute(value, 'dp', [(i, i ^ mask) for i in range(size)])]
  transfers between devices with their start and end apart: 24 -> 102, of which waited for: 21 -> 35; matrix products, arithmetic and copies ran while one was open for 10% -> 43% of each run, Pallas kernels for 0% -> 0%
where the time goes in v1:
time: 1150 us; the launch traced here: 1140 us
  waiting for transfers between devices  431 us (37%)
  matrix products  213 us (19%)
  starting transfers between devices  174 us (15%)
  other arithmetic  162 us (14%)
  local copies, waits for them, and re-layouts  155 us (13%)
    dot_general x39, matrix products, dot(): lax.dot_general(left, right, (contract, ((), ())), preferred_element_type...  200 us
    ppermute x40, waiting for transfers between devices, swap(): return lax.ppermute(value, 'dp', [(i, i ^ mask) for i in range(size)])  160 us
    ppermute x36, waiting for transfers between devices, shift(): return lax.ppermute(value, 'mp', [(i, (i + 1) % size) for i in range(size)])  96.8 us
    all_to_all x6, waiting for transfers between devices, spread(): lax.all_to_all(jnp.broadcast_to(value[None], (size,) + value.shape), axes...  80.3 us
    unnamed x402, local copies, waits for them, and re-layouts  52.9 us
    ppermute x40, starting transfers between devices, swap(): return lax.ppermute(value, 'dp', [(i, i ^ mask) for i in range(size)])  32.1 us
    all_to_all x6, starting transfers between devices, spread(): lax.all_to_all(jnp.broadcast_to(value[None], (size,) + value.shape), axes...  31.3 us
    ppermute x36, starting transfers between devices, shift(): return lax.ppermute(value, 'mp', [(i, (i + 1) % size) for i in range(size)])  29.3 us
  transfers between devices with their start and end apart: 102, of which 35 were waited for; matrix products, arithmetic and copies ran while one was open for 43% of the time, Pallas kernels for 0%

profile of v1, /device:TPU:4, one launch (start us, length us, event | category | flops | bytes accessed | tf_op | source)
XLA Modules:
  0.0 1141.3 jit_solution(8760595899430330454)
XLA Ops:
  99.2 11.9 %all-to-all-done.1 = bf16[4,64,1024]{2,1,0:T(8,128)(2,1)S(1)} async-done(((bf16[4,64,1024]{2,1,0:T(8,128)(2,1)}), bf16[4,64,1024]{2,1,0:T(8,128)(2,1)S(1)}, u32[]{:S(2)}, u32[]{:S(2)}) %all-to-all-start.1) | async-done | bytes 524320 | tf_op jit(solution)/shard_map/all_to_all | solution.py:247
  169.7 13.2 %collective-permute-done.4 = bf16[512,1024]{1,0:T(8,128)(2,1)} collective-permute-done((bf16[512,1024]{1,0:T(8,128)(2,1)}, bf16[512,1024]{1,0:T(8,128)(2,1)}, u32[]{:S(2)}, u32[]{:S(2)}) %collective-permute-start.4) | collective-permute-done | bytes 1048608 | tf_op jit(solution)/shard_map/ppermute | solution.py:45
  213.6 13.3 %all-to-all-done.3 = bf16[4,256,1024]{1,2,0:T(8,128)(2,1)} async-done(((bf16[4,256,1024]{1,2,0:T(8,128)(2,1)}), bf16[4,256,1024]{1,2,0:T(8,128)(2,1)}, u32[]{:S(2)}, u32[]{:S(2)}) %all-to-all-start.3) | async-done | bytes 2097184 | tf_op jit(solution)/shard_map/all_to_all | solution.py:119
  247.7 9.4 all-to-all-done.2
  284.1 14.0 %all-to-all-done.6 = bf16[4,50,1024]{2,1,0:T(8,128)(2,1)S(1)} async-done(((bf16[4,50,1024]{2,1,0:T(8,128)(2,1)}), bf16[4,50,1024]{2,1,0:T(8,128)(2,1)S(1)}, u32[]{:S(2)}, u32[]{:S(2)}) %all-to-all-start.6) | async-done | bytes 409632 | tf_op jit(solution)/shard_map/all_to_all | solution.py:151
  315.3 56.4 %all-to-all-done.7 = bf16[8,50,1024]{2,1,0:T(8,128)(2,1)} async-done(((bf16[8,50,1024]{2,1,0:T(8,128)(2,1)}), bf16[8,50,1024]{2,1,0:T(8,128)(2,1)}, u32[]{:S(2)}, u32[]{:S(2)}) %all-to-all-start.7) | async-done | bytes 819232 | tf_op jit(solution)/shard_map/all_to_all | solution.py:151
  427.2 11.3 collective-permute-done.18
  442.5 29.1 %all-to-all-done.12 = bf16[8,2,50,1024]{3,1,2,0:T(2,128)(2,1)} async-done(((bf16[8,2,50,1024]{3,1,2,0:T(2,128)(2,1)}), bf16[8,2,50,1024]{3,1,2,0:T(2,128)(2,1)}, u32[]{:S(2)}, u32[]{:S(2)}) %all-to-all-start.12) | async-done | bytes 1638432 | tf_op jit(solution)/shard_map/all_to_all | solution.py:362
  494.8 10.3 convolution_add_fusion.2
  515.0 9.9 collective-permute-done.21
  599.4 19.1 %fusion.8 = (bf16[2048,1024]{1,0:T(8,128)(2,1)}, bf16[2048,1024]{1,0:T(8,128)(2,1)}, bf16[2048,1024]{1,0:T(8,128)(2,1)}) fusion(f32[2048,1024]{1,0:T(8,128)} %convolution_add_fusion.2, f32[2048,1024]{1,0:T(8,128)} %convolution_add_fusion.3, f32[2048,1024]{1,0:T(8,128)} %fusion.245, bf16[2048,1024]{1,0:T(8,128)(2,1)S(1)} %bitcast.524, ...), kind=kOutput, calls=%fused_computation.24 | convolution fusion | flops 4351590400 | bytes 44040192 | tf_op jit(solution)/shard_map/dot_general | solution.py:19
  618.5 10.9 fusion.254
  672.3 8.6 convolution_convert_fusion
  724.8 29.9 %collective-permute-done.76 = bf16[1024,1024]{1,0:T(8,128)(2,1)} collective-permute-done((bf16[1024,1024]{1,0:T(8,128)(2,1)}, bf16[1024,1024]{1,0:T(8,128)(2,1)}, u32[]{:S(2)}, u32[]{:S(2)}) %collective-permute-start.76) | collective-permute-done | bytes 2097184 | tf_op jit(solution)/shard_map/ppermute | solution.py:45
  767.4 32.2 %collective-permute-done.75 = bf16[1024,1024]{1,0:T(8,128)(2,1)} collective-permute-done((bf16[1024,1024]{1,0:T(8,128)(2,1)}, bf16[1024,1024]{1,0:T(8,128)(2,1)}, u32[]{:S(2)}, u32[]{:S(2)}) %collective-permute-start.75) | collective-permute-done | bytes 2097184 | tf_op jit(solution)/shard_map/ppermute | solution.py:45
  809.9 34.2 %collective-permute-done.77 = bf16[1024,1024]{1,0:T(8,128)(2,1)} collective-permute-done((bf16[1024,1024]{1,0:T(8,128)(2,1)S(1)}, bf16[1024,1024]{1,0:T(8,128)(2,1)}, u32[]{:S(2)}, u32[]{:S(2)}) %collective-permute-start.77) | collective-permute-done | bytes 2097184 | tf_op jit(solution)/shard_map/ppermute | solution.py:45
  872.7 14.5 %collective-permute-done.56 = bf16[128,1024]{1,0:T(8,128)(2,1)} collective-permute-done((bf16[128,1024]{1,0:T(8,128)(2,1)S(1)}, bf16[128,1024]{1,0:T(8,128)(2,1)}, u32[]{:S(2)}, u32[]{:S(2)}) %collective-permute-start.56) | collective-permute-done | bytes 262176 | tf_op jit(solution)/shard_map/ppermute | solution.py:50
  923.1 9.5 collective-permute-done.30
  943.5 14.5 %collective-permute-done.59 = bf16[128,2048]{1,0:T(8,128)(2,1)} collective-permute-done((bf16[128,2048]{1,0:T(8,128)(2,1)}, bf16[128,2048]{1,0:T(8,128)(2,1)}, u32[]{:S(2)}, u32[]{:S(2)}) %collective-permute-start.59) | collective-permute-done | bytes 524320 | tf_op jit(solution)/shard_map/ppermute | solution.py:50
  989.2 9.7 collective-permute-done.61
  1027.9 14.0 %collective-permute-done.63 = bf16[128,2048]{1,0:T(8,128)(2,1)S(1)} collective-permute-done((bf16[128,2048]{1,0:T(8,128)(2,1)S(1)}, bf16[128,2048]{1,0:T(8,128)(2,1)S(1)}, u32[]{:S(2)}, u32[]{:S(2)}) %collective-permute-start.63) | collective-permute-done | bytes 524320 | tf_op jit(solution)/shard_map/ppermute | solution.py:50
  1043.3 12.5 %collective-permute-done.64 = bf16[128,2048]{1,0:T(8,128)(2,1)S(1)} collective-permute-done((bf16[128,2048]{1,0:T(8,128)(2,1)S(1)}, bf16[128,2048]{1,0:T(8,128)(2,1)S(1)}, u32[]{:S(2)}, u32[]{:S(2)}) %collective-permute-start.64) | collective-permute-done | bytes 524320 | tf_op jit(solution)/shard_map/ppermute | solution.py:50
  1079.9 14.1 %collective-permute-done.66 = bf16[512,1024]{1,0:T(8,128)(2,1)} collective-permute-done((bf16[512,1024]{1,0:T(8,128)(2,1)S(1)}, bf16[512,1024]{1,0:T(8,128)(2,1)}, u32[]{:S(2)}, u32[]{:S(2)}) %collective-permute-start.66) | collective-permute-done | bytes 1048608 | tf_op jit(solution)/shard_map/ppermute | solution.py:45
  1115.0 23.2 %collective-permute-done.71 = bf16[64,3072]{1,0:T(8,128)(2,1)S(1)} collective-permute-done((bf16[64,3072]{1,0:T(8,128)(2,1)S(1)}, bf16[64,3072]{1,0:T(8,128)(2,1)S(1)}, u32[]{:S(2)}, u32[]{:S(2)}) %collective-permute-start.71) | collective-permute-done | bytes 393248 | tf_op jit(solution)/shard_map/ppermute | solution.py:381
  (928 shorter events, 709.1 us)
Async XLA Ops:
  16.7 67.2 %collective-permute-start = (bf16[128,2048]{1,0:T(8,128)(2,1)}, bf16[128,2048]{1,0:T(8,128)(2,1)}, u32[]{:S(2)}, u32[]{:S(2)}) collective-permute-start(bf16[128,2048]{1,0:T(8,128)(2,1)} %constant_dynamic-update-slice_fusion), channel_id=1, source_target_pairs={{0,1},{1,2},{2,3},{3,0},{4,5},{5,6},{6,7},{7,4},{8,9},{9,10},{10,1... | collective-permute-start | bytes 1572872 | tf_op jit(solution)/shard_map/ppermute | solution.py:50
  25.6 93.1 %collective-permute-start.44 = (bf16[128,1024]{1,0:T(8,128)(2,1)}, bf16[128,1024]{1,0:T(8,128)(2,1)}, u32[]{:S(2)}, u32[]{:S(2)}) collective-permute-start(bf16[128,1024]{1,0:T(8,128)(2,1)} %get-tuple-element.188), channel_id=1, source_target_pairs={{0,8},{4,12},{8,0},{12,4},{16,24},{20,28},{24,16},{28,20},{1,9},{5... | collective-permute-start | bytes 786440 | tf_op jit(solution)/shard_map/ppermute | solution.py:45
  26.8 95.5 %collective-permute-start.39 = (bf16[128,1024]{1,0:T(8,128)(2,1)}, bf16[128,1024]{1,0:T(8,128)(2,1)}, u32[]{:S(2)}, u32[]{:S(2)}) collective-permute-start(bf16[128,1024]{1,0:T(8,128)(2,1)} %get-tuple-element.187), channel_id=1, source_target_pairs={{0,1},{1,2},{2,3},{3,0},{4,5},{5,6},{6,7},{7,4},{8,9},{9,10},{10,1... | collective-permute-start | bytes 786440 | tf_op jit(solution)/shard_map/ppermute | solution.py:50
  160.8 101.9 %collective-permute-start.41 = (bf16[128,1024]{1,0:T(8,128)(2,1)}, bf16[128,1024]{1,0:T(8,128)(2,1)}, u32[]{:S(2)}, u32[]{:S(2)}) collective-permute-start(bf16[128,1024]{1,0:T(8,128)(2,1)} %collective-permute-done.40), channel_id=1, source_target_pairs={{0,1},{1,2},{2,3},{3,0},{4,5},{5,6},{6,7},{7,4},{8,9},{9,10},{10,1... | collective-permute-start | bytes 786440 | tf_op jit(solution)/shard_map/ppermute | solution.py:50
  162.5 103.2 %collective-permute-start.46 = (bf16[2,128,1024]{2,1,0:T(8,128)(2,1)}, bf16[2,128,1024]{2,1,0:T(8,128)(2,1)}, u32[]{:S(2)}, u32[]{:S(2)}) collective-permute-start(bf16[2,128,1024]{2,1,0:T(8,128)(2,1)} %collective-permute-done.45), channel_id=1, source_target_pairs={{0,1},{1,2},{2,3},{3,0},{4,5},{5,6},{6,7},{7,4},{8,9},{9,10},{10,1... | collective-permute-start | bytes 1572872 | tf_op jit(solution)/shard_map/ppermute | solution.py:50
  270.3 145.5 %collective-permute-start.25 = (bf16[1024,1024]{1,0:T(8,128)(2,1)}, bf16[1024,1024]{1,0:T(8,128)(2,1)}, u32[]{:S(2)}, u32[]{:S(2)}) collective-permute-start(bf16[1024,1024]{1,0:T(8,128)(2,1)} %bitcast.541), channel_id=1, source_target_pairs={{0,16},{4,20},{8,24},{12,28},{16,0},{20,4},{24,8},{28,12},{1,17},{... | collective-permute-start | bytes 6291464 | tf_op jit(solution)/shard_map/ppermute | solution.py:45
  275.9 298.9 %collective-permute-start.24 = (bf16[1024,1024]{1,0:T(8,128)(2,1)}, bf16[1024,1024]{1,0:T(8,128)(2,1)}, u32[]{:S(2)}, u32[]{:S(2)}) collective-permute-start(bf16[1024,1024]{1,0:T(8,128)(2,1)} %bitcast.34), channel_id=1, source_target_pairs={{0,16},{4,20},{8,24},{12,28},{16,0},{20,4},{24,8},{28,12},{1,17},{... | collective-permute-start | bytes 6291464 | tf_op jit(solution)/shard_map/ppermute | solution.py:45
  300.0 71.7 %all-to-all-start.7 = ((bf16[8,50,1024]{2,1,0:T(8,128)(2,1)}), bf16[8,50,1024]{2,1,0:T(8,128)(2,1)}, u32[]{:S(2)}, u32[]{:S(2)}) async-start(bf16[8,50,1024]{2,1,0:T(8,128)(2,1)} %broadcast_in_dim.68), calls=%async_computation.7 | async-start | bytes 1835008 | tf_op jit(solution)/shard_map/all_to_all | solution.py:151
  309.6 96.7 %collective-permute-start.48 = (bf16[2,4,128,1024]{3,2,0,1:T(8,128)(2,1)}, bf16[2,4,128,1024]{3,2,0,1:T(8,128)(2,1)}, u32[]{:S(2)}, u32[]{:S(2)}) collective-permute-start(bf16[2,4,128,1024]{3,2,0,1:T(8,128)(2,1)} %get-tuple-element.167), channel_id=1, source_target_pairs={{0,4},{4,0},{8,12},{12,8},{16,20},{20,16},{24,28},{28,24},{1,5},{5... | collective-permute-start | bytes 6291464 | tf_op jit(solution)/shard_map/ppermute | solution.py:45
  312.7 163.2 %collective-permute-start.43 = (bf16[2,4,128,1024]{3,2,1,0:T(8,128)(2,1)}, bf16[2,4,128,1024]{3,2,1,0:T(8,128)(2,1)}, u32[]{:S(2)}, u32[]{:S(2)}) collective-permute-start(bf16[2,4,128,1024]{3,2,1,0:T(8,128)(2,1)} %get-tuple-element.165), channel_id=1, source_target_pairs={{0,4},{4,0},{8,12},{12,8},{16,20},{20,16},{24,28},{28,24},{1,5},{5... | collective-permute-start | bytes 6291464 | tf_op jit(solution)/shard_map/ppermute | solution.py:45
  315.3 77.2 %collective-permute-start.12 = (bf16[128,2048]{1,0:T(8,128)(2,1)}, bf16[128,2048]{1,0:T(8,128)(2,1)}, u32[]{:S(2)}, u32[]{:S(2)}) collective-permute-start(bf16[128,2048]{1,0:T(8,128)(2,1)} %fusion.64), channel_id=1, source_target_pairs={{0,1},{1,2},{2,3},{3,0},{4,5},{5,6},{6,7},{7,4},{8,9},{9,10},{10,1... | collective-permute-start | bytes 1572872 | tf_op jit(solution)/shard_map/ppermute | solution.py:50
  406.3 184.7 %collective-permute-start.23 = (bf16[1024,1024]{1,0:T(8,128)(2,1)}, bf16[1024,1024]{1,0:T(8,128)(2,1)}, u32[]{:S(2)}, u32[]{:S(2)}) collective-permute-start(bf16[1024,1024]{1,0:T(8,128)(2,1)} %bitcast.22), channel_id=1, source_target_pairs={{0,16},{4,20},{8,24},{12,28},{16,0},{20,4},{24,8},{28,12},{1,17},{... | collective-permute-start | bytes 6291464 | tf_op jit(solution)/shard_map/ppermute | solution.py:45
  406.3 65.2 %all-to-all-start.12 = ((bf16[8,2,50,1024]{3,1,2,0:T(2,128)(2,1)}), bf16[8,2,50,1024]{3,1,2,0:T(2,128)(2,1)}, u32[]{:S(2)}, u32[]{:S(2)}) async-start(bf16[8,2,50,1024]{3,1,2,0:T(2,128)(2,1)} %copy.502), calls=%async_computation.12 | async-start | bytes 3276800 | tf_op jit(solution)/shard_map/all_to_all | solution.py:362
  515.0 53.6 %collective-permute-start.17 = (bf16[2,4,128,1024]{3,2,1,0:T(8,128)(2,1)}, bf16[2,4,128,1024]{3,2,1,0:T(8,128)(2,1)}, u32[]{:S(2)}, u32[]{:S(2)}) collective-permute-start(bf16[2,4,128,1024]{3,2,1,0:T(8,128)(2,1)} %get-tuple-element.169), channel_id=1, source_target_pairs={{0,4},{4,0},{8,12},{12,8},{16,20},{20,16},{24,28},{28,24},{1,5},{5... | collective-permute-start | bytes 6291464 | tf_op jit(solution)/shard_map/ppermute | solution.py:45
  568.1 121.6 %collective-permute-start.73 = (bf16[256,1024]{1,0:T(8,128)(2,1)}, bf16[256,1024]{1,0:T(8,128)(2,1)}, u32[]{:S(2)}, u32[]{:S(2)}) collective-permute-start(bf16[256,1024]{1,0:T(8,128)(2,1)} %slice.1346), channel_id=1, source_target_pairs={{0,8},{4,12},{8,0},{12,4},{16,24},{20,28},{24,16},{28,20},{1,9},{5... | collective-permute-start | bytes 1572872 | tf_op jit(solution)/shard_map/ppermute | solution.py:45
  655.7 61.4 %collective-permute-start.49 = (bf16[2,4,128,1024]{3,2,0,1:T(8,128)(2,1)}, bf16[2,4,128,1024]{3,2,0,1:T(8,128)(2,1)S(1)}, u32[]{:S(2)}, u32[]{:S(2)}) collective-permute-start(bf16[2,4,128,1024]{3,2,0,1:T(8,128)(2,1)} %copy.505), channel_id=1, source_target_pairs={{0,4},{4,0},{8,12},{12,8},{16,20},{20,16},{24,28},{28,24},{1,5},{5... | collective-permute-start | bytes 6291464 | tf_op jit(solution)/shard_map/ppermute | solution.py:45
  705.9 57.5 %collective-permute-start.31 = (bf16[2,4,128,1024]{3,2,1,0:T(8,128)(2,1)}, bf16[2,4,128,1024]{3,2,1,0:T(8,128)(2,1)}, u32[]{:S(2)}, u32[]{:S(2)}) collective-permute-start(bf16[2,4,128,1024]{3,2,1,0:T(8,128)(2,1)} %bitcast.48), channel_id=1, source_target_pairs={{0,4},{4,0},{8,12},{12,8},{16,20},{20,16},{24,28},{28,24},{1,5},{5... | collective-permute-start | bytes 6291464 | tf_op jit(solution)/shard_map/ppermute | solution.py:45
  709.1 149.6 %all-to-all-start.17 = ((bf16[4,32,1024]{2,1,0:T(8,128)(2,1)}), bf16[4,32,1024]{2,1,0:T(8,128)(2,1)S(1)}, u32[]{:S(2)}, u32[]{:S(2)}) async-start(bf16[4,32,1024]{2,1,0:T(8,128)(2,1)} %bitcast.552), calls=%async_computation.17 | async-start | bytes 524288 | tf_op jit(solution)/shard_map/all_to_all | solution.py:394
  712.5 87.1 %collective-permute-start.75 = (bf16[1024,1024]{1,0:T(8,128)(2,1)}, bf16[1024,1024]{1,0:T(8,128)(2,1)}, u32[]{:S(2)}, u32[]{:S(2)}) collective-permute-start(bf16[1024,1024]{1,0:T(8,128)(2,1)} %convolution_convert_fusion.2), channel_id=1, source_target_pairs={{0,16},{4,20},{8,24},{12,28},{16,0},{20,4},{24,8},{28,12},{1,17},{... | collective-permute-start | bytes 6291464 | tf_op jit(solution)/shard_map/ppermute | solution.py:45
  717.1 127.1 %collective-permute-start.77 = (bf16[1024,1024]{1,0:T(8,128)(2,1)S(1)}, bf16[1024,1024]{1,0:T(8,128)(2,1)}, u32[]{:S(2)}, u32[]{:S(2)}) collective-permute-start(bf16[1024,1024]{1,0:T(8,128)(2,1)S(1)} %copy-done.177), channel_id=1, source_target_pairs={{0,16},{4,20},{8,24},{12,28},{16,0},{20,4},{24,8},{28,12},{1,17},{... | collective-permute-start | bytes 6291464 | tf_op jit(solution)/shard_map/ppermute | solution.py:45
  719.7 90.0 %collective-permute-start.50 = (bf16[2,128,1024]{2,1,0:T(8,128)(2,1)S(1)}, bf16[2,128,1024]{2,1,0:T(8,128)(2,1)S(1)}, u32[]{:S(2)}, u32[]{:S(2)}) collective-permute-start(bf16[2,128,1024]{2,1,0:T(8,128)(2,1)S(1)} %fusion.87), channel_id=1, source_target_pairs={{0,1},{1,2},{2,3},{3,0},{4,5},{5,6},{6,7},{7,4},{8,9},{9,10},{10,1... | collective-permute-start | bytes 1572872 | tf_op jit(solution)/shard_map/ppermute | solution.py:50
  754.7 99.9 %collective-permute-start.55 = (bf16[4,128,1024]{2,1,0:T(8,128)(2,1)S(1)}, bf16[4,128,1024]{2,1,0:T(8,128)(2,1)S(1)}, u32[]{:S(2)}, u32[]{:S(2)}) collective-permute-start(bf16[4,128,1024]{2,1,0:T(8,128)(2,1)S(1)} %fusion.50), channel_id=1, source_target_pairs={{0,8},{4,12},{8,0},{12,4},{16,24},{20,28},{24,16},{28,20},{1,9},{5... | collective-permute-start | bytes 3145736 | tf_op jit(solution)/shard_map/ppermute | solution.py:45
  763.5 89.0 %collective-permute-start.27 = (bf16[2,128,1024]{2,1,0:T(8,128)(2,1)S(1)}, bf16[2,128,1024]{2,1,0:T(8,128)(2,1)S(1)}, u32[]{:S(2)}, u32[]{:S(2)}) collective-permute-start(bf16[2,128,1024]{2,1,0:T(8,128)(2,1)S(1)} %fusion.86), channel_id=1, source_target_pairs={{0,1},{1,2},{2,3},{3,0},{4,5},{5,6},{6,7},{7,4},{8,9},{9,10},{10,1... | collective-permute-start | bytes 1572872 | tf_op jit(solution)/shard_map/ppermute | solution.py:50
  799.6 63.4 %collective-permute-start.32 = (bf16[4,128,1024]{2,1,0:T(8,128)(2,1)}, bf16[4,128,1024]{2,1,0:T(8,128)(2,1)S(1)}, u32[]{:S(2)}, u32[]{:S(2)}) collective-permute-start(bf16[4,128,1024]{2,1,0:T(8,128)(2,1)} %fusion.49), channel_id=1, source_target_pairs={{0,8},{4,12},{8,0},{12,4},{16,24},{20,28},{24,16},{28,20},{1,9},{5... | collective-permute-start | bytes 3145736 | tf_op jit(solution)/shard_map/ppermute | solution.py:45
  (274 other events, 4789.1 us)

commit v2 on v1

v2 whole, which is shorter than its diff:
```python
import functools
import math

import jax
import jax.numpy as jnp
from jax import lax
from jax.experimental import pallas as pl
from jax.experimental.pallas import tpu as pltpu
from jax.sharding import PartitionSpec as P

HEADS = 8
HD = 256
WIDTH_Q = HEADS * HD
INNER = 4
BF = jnp.bfloat16
F32 = jnp.float32

EPS = 1e-06


def dot(left, right, contract):
    return lax.dot_general(left, right, (contract, ((), ())), preferred_element_type=F32)


def mm(left, right):
    return dot(left, right, ((1,), (0,)))


def mm_nt(left, right):
    return dot(left, right, ((1,), (1,)))


def mm_tn(left, right):
    return dot(left, right, ((0,), (0,)))


def tie(*values):
    return lax.optimization_barrier(values)


def normed(values, gain):
    scale = lax.rsqrt(jnp.mean(values * values, axis=-1, keepdims=True) + EPS)
    return values * scale * gain


def geglu(gate, up_part):
    return jax.nn.gelu(gate, approximate=True) * up_part


def swap(value, mask):
    size = lax.axis_size("dp")
    return lax.ppermute(value, "dp", [(i, i ^ mask) for i in range(size)])


def bit_of(mask):
    return (lax.axis_index("dp") // mask) % 2


def join(own, other, bit, axis):
    shape = [1] * (own.ndim + 1)
    shape[axis] = 2
    here = (jnp.arange(2, dtype=jnp.int32) == bit).reshape(shape)
    return jnp.where(here, jnp.expand_dims(own, axis), jnp.expand_dims(other, axis))


def dp_gather(value, masks, done=()):
    done = list(done)
    for mask in masks:
        axis = sum(m > mask for m in done)
        value = join(value, swap(value, mask), bit_of(mask), axis)
        done.append(mask)
    return value


def dp_scatter(value, masks, steps=None):
    left = list(masks)
    end = len(left) - steps if steps else 0
    while len(left) > end:
        mask = left.pop()
        axis = sum(m > mask for m in left)
        bit = bit_of(mask)
        other = lax.dynamic_index_in_dim(value, 1 - bit, axis, keepdims=False).astype(BF)
        own = lax.dynamic_index_in_dim(value, bit, axis, keepdims=False)
        value = own.astype(F32) + swap(other, mask).astype(F32)
    return value


def exchange(value, axes="mp"):
    return lax.all_to_all(value, axes, 0, 0, tiled=True)


def spread(value):
    return exchange(jnp.broadcast_to(value[None], (lax.axis_size("mp"),) + value.shape))


def shift(value, steps):
    size = lax.axis_size("mp")
    return lax.ppermute(value, "mp", [(i, (i + steps) % size) for i in range(size)])


def ring(value):
    return [value] + [shift(value, s) for s in range(1, lax.axis_size("mp"))]


def unring(blocks, axis):
    size = blocks[0].shape[axis]
    twice = jnp.concatenate((blocks[:1] + blocks[:0:-1]) * 2, axis=axis)
    count = len(blocks)
    start = (count - lax.axis_index("mp")) % count * size
    return lax.dynamic_slice_in_dim(twice, start, count * size, axis)


def fold(rows_a, width):
    times = width // rows_a.shape[-1]
    n = rows_a.shape[-2] // times
    return jnp.concatenate([rows_a[..., i * n : (i + 1) * n, :] for i in range(times)], axis=-1)


def unfold(rows, width):
    times = rows.shape[-1] // width
    return jnp.concatenate(
        [rows[..., i * width : (i + 1) * width] for i in range(times)], axis=-2
    )


def tokens_of(blocks, slab, width_a):
    prefix = jnp.concatenate([block[:, :slab].reshape(-1, block.shape[2]) for block in blocks])
    action = jnp.concatenate([block[:, slab:].reshape(-1, block.shape[2]) for block in blocks])
    return prefix, unfold(action, width_a)


def sum_cores(prefix, action, slab):
    shard_count = lax.axis_size("mp")
    prefix = prefix.reshape(4, shard_count, slab, -1)
    action = fold(action, prefix.shape[-1]).reshape(4, shard_count, -1, prefix.shape[-1])
    near, far, near_core, far_core = [
        jnp.concatenate([prefix[k], action[k]], axis=1) for k in range(4)
    ]
    far = (far.astype(F32) + swap(far_core, 1).astype(F32)).astype(BF)
    near = (near.astype(F32) + swap(near_core, 1).astype(F32)).astype(BF)
    return near, far


def ffn_kernel(
    places_ref,
    h_ref,
    g_ref,
    *refs,
    pieces_up,
    pieces_down,
):
    up_refs = refs[:pieces_up]
    down_refs = refs[pieces_up : pieces_up + pieces_down]
    act_ref, d_both_ref, dh_ref, gate_up, down, sems = refs[pieces_up + pieces_down :]

    @pl.when(pl.program_id(0) == 0)
    def _():
        copies = []
        rows = gate_up.shape[0] // pieces_up
        for j, ref in enumerate(up_refs):
            place = places_ref[j] if pieces_up > 1 else 0
            target = gate_up.at[pl.ds(pl.multiple_of(place * rows, rows), rows)]
            copies.append(pltpu.make_async_copy(ref, target, sems.at[j]))
        for j, ref in enumerate(down_refs):
            place = places_ref[j] if pieces_down > 1 else 0
            copies.append(pltpu.make_async_copy(ref, down.at[place], sems.at[pieces_up + j]))
        for copy in copies:
            copy.start()
        for copy in copies:
            copy.wait()

    hidden = act_ref.shape[1]
    both = mm(h_ref[...], gate_up[...])
    gate, up_part = both[:, :hidden], both[:, hidden:]
    d_act = jnp.zeros(gate.shape, F32)
    width = down.shape[2]
    for k in range(pieces_down):
        d_act = d_act + mm_nt(g_ref[:, k * width : (k + 1) * width], down[k])
    root = math.sqrt(2.0 / math.pi)
    square = gate * gate
    tanh = jnp.tanh(root * gate * (1.0 + 0.044715 * square))
    plus = 0.5 * (1.0 + tanh)
    gelu = gate * plus
    slope = plus + 0.5 * gate * (1.0 - tanh * tanh) * (root * (1.0 + 3 * 0.044715 * square))
    act_ref[...] = (gelu * up_part).astype(BF)
    d_both_ref[:, :hidden] = (d_act * up_part * slope).astype(BF)
    d_both_ref[:, hidden:] = (d_act * gelu).astype(BF)
    dh_ref[...] = mm_nt(d_both_ref[...], gate_up[...]).astype(BF)


def feed_forward(h, g, places, up_pieces, down_pieces):
    tokens, width = h.shape
    block = min(tokens, 256)
    hidden = down_pieces[0].shape[0]
    count_up, count_down = len(up_pieces), len(down_pieces)

    def rows(columns):
        return pl.BlockSpec((block, columns), lambda i, places: (i, 0))

    return pl.pallas_call(
        functools.partial(ffn_kernel, pieces_up=count_up, pieces_down=count_down),
        grid_spec=pltpu.PrefetchScalarGridSpec(
            num_scalar_prefetch=1,
            grid=(tokens // block,),
            in_specs=[rows(width), rows(width)]
            + [pl.BlockSpec(memory_space=pl.ANY)] * (count_up + count_down),
            out_specs=[rows(hidden), rows(2 * hidden), rows(width)],
            scratch_shapes=[
                pltpu.VMEM((width, 2 * hidden), BF),
                pltpu.VMEM((count_down,) + down_pieces[0].shape, BF),
                pltpu.SemaphoreType.DMA((count_up + count_down,)),
            ],
        ),
        out_shape=[
            jax.ShapeDtypeStruct((tokens, hidden), BF),
            jax.ShapeDtypeStruct((tokens, 2 * hidden), BF),
            jax.ShapeDtypeStruct((tokens, width), BF),
        ],
        compiler_params=pltpu.CompilerParams(vmem_limit_bytes=44 * 2**20),
        name="ffn",
    )(places, h, g, *up_pieces, *down_pieces)


def down_kernel(places_ref, act_ref, *refs):
    down_refs, out_ref = refs[:-1], refs[-1]
    width = out_ref.shape[1] // len(down_refs)
    for j, ref in enumerate(down_refs):
        place = pl.multiple_of(places_ref[j] * width, width)
        out_ref[:, pl.ds(place, width)] = mm(act_ref[...], ref[...]).astype(BF)


def down_product(act, places, down_pieces):
    tokens, hidden = act.shape
    block = min(tokens, 512)
    width = len(down_pieces) * down_pieces[0].shape[1]
    whole = pl.BlockSpec(down_pieces[0].shape, lambda i, places: (0, 0))
    return pl.pallas_call(
        down_kernel,
        grid_spec=pltpu.PrefetchScalarGridSpec(
            num_scalar_prefetch=1,
            grid=(tokens // block,),
            in_specs=[pl.BlockSpec((block, hidden), lambda i, places: (i, 0))]
            + [whole] * len(down_pieces),
            out_specs=pl.BlockSpec((block, width), lambda i, places: (i, 0)),
        ),
        out_shape=jax.ShapeDtypeStruct((tokens, width), BF),
        compiler_params=pltpu.CompilerParams(vmem_limit_bytes=32 * 2**20),
        name="down",
    )(places, act, *down_pieces)


def rows_of_heads(values):
    return jnp.concatenate(
        [values[:, i : i + HD] for i in range(0, values.shape[1], HD)], axis=0
    )


def heads_of_rows(values, heads):
    n = values.shape[0] // heads
    return jnp.concatenate([values[i * n : (i + 1) * n] for i in range(heads)], axis=1)


def on_device(
    prefix_in,
    action_in,
    prefix_len,
    action_count,
    loss_weight,
    prefix_gains,
    action_gains,
    prefix_qkv,
    prefix_out_proj,
    action_qkv,
    action_out_proj,
    prefix_gate_up,
    prefix_down,
    action_gate_up,
    action_down,
    prefix_cot,
    action_cot,
):
    dp = lax.axis_index("dp")
    z = lax.axis_index("mp")
    dp_count = lax.axis_size("dp")
    shard_count = lax.axis_size("mp")
    slab = prefix_in.shape[1]
    width_p = prefix_in.shape[2]
    width_a = action_in.shape[2]
    action_rows = action_in.shape[1]
    whole_len = slab * shard_count
    query_here = WIDTH_Q // shard_count
    heads_here = query_here // HD
    slab_a = -(-action_rows // (16 * shard_count)) * 16
    whole_a = slab_a * shard_count
    outer_masks = []
    mask = INNER
    while mask < dp_count:
        outer_masks.append(mask)
        mask *= 2
    masks_p = [2] + outer_masks + [1]
    masks_a = outer_masks + [2] + [1]
    everywhere = ("dp", "mp")
    cut = width_p * 5 // 8
    total = dp_count * shard_count
    outer = dp_count // INNER
    inner = dp % INNER

    rows_qp = prefix_qkv.shape[0]
    width_kv = query_here + 2 * HD
    own_gain_p = prefix_gains[:, :1].astype(F32)
    own_gain_a = action_gains[:, :1].astype(F32)
    both = jnp.concatenate(
        [prefix_qkv.astype(F32) * own_gain_p, action_qkv.astype(F32) * own_gain_a], axis=0
    ).astype(BF)
    both = jnp.stack(
        [
            jnp.concatenate(
                [both[:, k * query_here : (k + 1) * query_here], both[:, WIDTH_Q:]], axis=1
            )
            for k in range(shard_count)
        ]
    )
    gains_own = jnp.concatenate([prefix_gains[:, 1], action_gains[:, 1]])
    gains_own = jnp.pad(gains_own[None], ((0, 7), (0, width_kv - gains_own.shape[0])))
    both = jnp.concatenate(
        [both, jnp.broadcast_to(gains_own[None], (shard_count,) + gains_own.shape)], axis=1
    )
    both = exchange(both)
    to_heads = [(j, (j % dp_count) * shard_count + j // dp_count) for j in range(total)]
    from_heads = [(b, a) for a, b in to_heads]
    out_own = jnp.concatenate([prefix_out_proj, action_out_proj], axis=1)
    out_own = lax.ppermute(out_own, everywhere, to_heads)
    hidden_p = prefix_down.shape[0] // INNER
    hidden_a = action_down.shape[0] // INNER
    rows_p = prefix_down.shape[1]
    rows_a = action_down.shape[1]

    side, core = bit_of(2), dp % 2

    def half_columns(values, hidden, at):
        gate, up_part = [
            lax.dynamic_slice_in_dim(w, at * 2 * hidden, 2 * hidden, 1) for w in values
        ]
        return jnp.concatenate(
            [gate[:, :hidden], up_part[:, :hidden], gate[:, hidden:], up_part[:, hidden:]], axis=1
        )

    def gate_up_part(at):
        return half_columns(prefix_gate_up, hidden_p, at)

    def down_part(at):
        return lax.dynamic_slice_in_dim(prefix_down, at * 2 * hidden_p, 2 * hidden_p, 0)

    def small_part(at):
        up = half_columns(action_gate_up, hidden_a, at)
        down = lax.dynamic_slice_in_dim(action_down, at * 2 * hidden_a, 2 * hidden_a, 0)
        down = unfold_rows(down.reshape(2, hidden_a, rows_a))
        return jnp.concatenate(
            [up[:, : 2 * hidden_a], down[0], up[:, 2 * hidden_a :], down[1]], axis=1
        )

    def widen(piece):
        pieces = [piece]
        for mask in outer_masks:
            pieces = pieces + [swap(p, mask) for p in pieces]
        return pieces

    def for_cores(piece, axis):
        size = piece.shape[axis] // 2
        own = lax.dynamic_slice_in_dim(piece, core * size, size, axis)
        other = lax.dynamic_slice_in_dim(piece, (1 - core) * size, size, axis)
        return [own, swap(other, 1)]

    keep_prefix = jnp.arange(whole_len, dtype=jnp.int32) < prefix_len[0]
    keep_action = jnp.arange(whole_a, dtype=jnp.int32) < action_count[0]
    weight = loss_weight[0].astype(F32)
    own_p = z * slab + jnp.arange(slab, dtype=jnp.int32) < prefix_len[0]
    own_a = z * slab_a + jnp.arange(slab_a, dtype=jnp.int32) < action_count[0]

    def own_rows_a(values):
        padded = jnp.pad(values[0], ((0, whole_a - action_rows), (0, 0)))
        return padded, lax.dynamic_slice_in_dim(padded, z * slab_a, slab_a, 0)

    _, cot_a = own_rows_a(action_cot)
    grad_out_p = prefix_cot[0].astype(F32) * (weight * own_p.astype(F32))[:, None]
    grad_out_a = cot_a.astype(F32) * (weight * own_a.astype(F32))[:, None]
    x_a, x_own_a = own_rows_a(action_in)
    input_p = prefix_in[0].astype(F32)
    input_a = x_own_a.astype(F32)

    def packed(values_p, values_a):
        return jnp.concatenate([values_p.astype(BF), fold(values_a.astype(BF), width_p)], axis=-2)

    def unpacked(rows):
        return rows[..., :slab, :], unfold(rows[..., slab:, :], width_a)

    down_far, down_near = swap(down_part(1 - side), 2), widen(down_part(side))
    both, out_own, x_all = tie(both, out_own, prefix_in[0])
    x_all = spread(x_all)
    value = both[:, :rows_qp].reshape(-1, width_kv)
    value_a = both[:, rows_qp:].reshape(-1, width_kv)
    out_both = join(out_own, swap(out_own, masks_a[0]), bit_of(masks_a[0]), 0)
    other, down_far, down_near, value_a, out_both = tie(
        swap(value, 2), down_far, down_near, value_a, out_both
    )
    value = join(value, other, bit_of(2), 0)
    done = [2]
    for mask in outer_masks:
        axis = sum(m > mask for m in done)
        value = join(value, swap(value, mask), bit_of(mask), axis)
        done.append(mask)
    value_a = dp_gather(value_a, masks_a[:-1])
    out_both = dp_gather(out_both, masks_a[1:-1], masks_a[:1])
    value, value_a, x_all, out_both, prefix_gate_up, action_gate_up, action_down = tie(
        value, value_a, x_all, out_both, prefix_gate_up, action_gate_up, action_down
    )
    value_a = dp_gather(value_a, [1], masks_a[:-1]).reshape(total, -1, width_kv)
    rows_qa = action_qkv.shape[0]
    qkv_a = value_a[:, :rows_qa].reshape(-1, width_kv)
    gains = value_a[:, rows_qa].astype(F32)
    gain_ffn_p = gains[:, :rows_qp].reshape(-1)
    gain_ffn_a = gains[:, rows_qp : rows_qp + rows_qa].reshape(-1)
    qkv_p = join(value, swap(value, 1), bit_of(1), len(done)).reshape(-1, width_kv)
    out_both = dp_gather(out_both, [1], masks_a[:-1]).reshape(-1, width_p + width_a)
    out_p = out_both[:, :width_p]
    out_a = out_both[:, width_p:]
    up_far, up_near = swap(gate_up_part(1 - side), 2), widen(gate_up_part(side))
    x_all, g_rows = tie(x_all, packed(grad_out_p, grad_out_a))
    g_near = spread(g_rows)

    def slab_terms(terms_p, terms_a):
        return exchange(
            packed(
                terms_p.reshape(shard_count, slab, width_p),
                terms_a.reshape(shard_count, slab_a, width_a),
            )
        )

    def sum_slabs(terms):
        return unpacked(jnp.sum(terms.astype(F32), axis=0))

    h_attn_p = normed(x_all.reshape(whole_len, width_p).astype(F32), 1.0).astype(BF)
    h_attn_a = normed(x_a.astype(F32), 1.0).astype(BF)
    all_p = mm(h_attn_p, qkv_p).astype(BF)
    all_a = mm(h_attn_a, qkv_a).astype(BF)
    query = jnp.concatenate(
        [rows_of_heads(all_p[:, :query_here]), rows_of_heads(all_a[:, :query_here])]
    )
    kv = jnp.concatenate([all_p[:, query_here:], all_a[:, query_here:]])
    keys, vals = kv[:, :HD], kv[:, HD:]
    split = heads_here * whole_len
    is_action = jnp.arange(query.shape[0], dtype=jnp.int32) >= split
    keep = jnp.concatenate([keep_prefix, keep_action])
    keep = keep[None, :] & (
        is_action[:, None] | (jnp.arange(kv.shape[0], dtype=jnp.int32) < whole_len)[None, :]
    )
    scale = 1.0 / math.sqrt(HD)
    scores = jnp.where(keep, mm_nt(query, keys) * scale, -1e30)
    probs = jnp.exp(scores - jnp.max(scores, axis=-1, keepdims=True))
    probs = probs / jnp.sum(probs, axis=-1, keepdims=True)
    probs_low = probs.astype(BF)
    mixed = mm(probs_low, vals).astype(BF)
    mixed, up_far, up_near, g_near, down_far = tie(mixed, up_far, up_near, g_near, down_far)
    up_far = widen(up_far)
    g_far = swap(g_near, 2)
    small_far, small_near = swap(small_part(1 - side), 2), widen(small_part(side))
    mixed_p = heads_of_rows(mixed[:split], heads_here)
    mixed_a = heads_of_rows(mixed[split:], heads_here)
    mid = slab_terms(mm(mixed_p, out_p), mm(mixed_a, out_a))
    mid, small_far, small_near, down_far = tie(mid, small_far, small_near, down_far)
    small_far, down_far = widen(small_far), widen(down_far)
    mid_p, mid_a = sum_slabs(mid)
    mid_p = input_p + mid_p
    mid_a = input_a + mid_a

    h_rows = packed(normed(mid_p, gain_ffn_p), normed(mid_a, gain_ffn_a))
    near = jnp.stack([h_rows[:, cut:], swap(h_rows[:, cut:], 2)])
    first = spread(h_rows[:, :cut])
    first, near, up_far, g_far, small_far = tie(first, near, up_far, g_far, small_far)
    second = spread(near)
    first_far = swap(first, 2)
    ups = [for_cores(up_near[k], 1) + for_cores(up_far[k], 1) for k in range(outer)]
    g_p, g_a = tokens_of([g_near, g_far, swap(g_near, 1), swap(g_far, 1)], slab, width_a)
    first_core = swap(first, 1)
    second, g_p, g_a, ups, down_far, first_core, first_far = tie(
        second, g_p, g_a, ups, down_far, first_core, first_far
    )
    second_core = swap(second, 1)
    pairs = [
        (first, second[:, 0]),
        (first_far, second[:, 1]),
        (first_core, second_core[:, 0]),
        (swap(first_far, 1), second_core[:, 1]),
    ]
    h_p, h_a = tokens_of([jnp.concatenate(pair, axis=2) for pair in pairs], slab, width_a)
    downs, smalls = [], []
    for k in range(outer):
        downs += for_cores(down_near[k], 0) + for_cores(down_far[k], 0)
        smalls += for_cores(small_near[k], 1) + for_cores(small_far[k], 1)
    small = jnp.stack(smalls)
    bit = 1
    while bit < dp_count:
        pairs = small.reshape((dp_count // (2 * bit), 2, bit) + small.shape[1:])
        small = jnp.where((dp & bit) != 0, pairs[:, ::-1], pairs).reshape(small.shape)
        bit *= 2
    gate_up_a = small[:, :, : 2 * hidden_a].reshape(width_a, 2 * hidden_a)
    down_a = fold_rows(small[:, :, 2 * hidden_a :], rows_a)
    down_a = down_a.transpose(1, 0, 2).reshape(hidden_a, width_a)
    places = dp ^ jnp.arange(dp_count, dtype=jnp.int32)
    gate_up_pieces = [piece for k in range(outer) for piece in ups[k]]
    down_pieces = downs
    act_p, d_both_p, dh_p = feed_forward(h_p, g_p, places, gate_up_pieces, down_pieces)
    act_a, d_both_a, dh_a = feed_forward(h_a, g_a, places, [gate_up_a], [down_a])
    half = outer // 2

    def send_outer(terms):
        return [swap(terms[k], half * INNER) for k in sorted(terms)]

    def sum_outer(terms, got):
        terms = [terms[k] + got[k].astype(F32) for k in sorted(terms)]
        size = half
        while size > 1:
            size //= 2
            terms = [
                terms[k] + swap(terms[k + size].astype(BF), size * INNER).astype(F32)
                for k in range(size)
            ]
        return terms[0].astype(BF)

    def side_columns(values, k, far):
        width = values.shape[1] // dp_count
        place = ((dp ^ (k * INNER) ^ far) // 2) * 2 * width
        return lax.dynamic_slice_in_dim(values, place, 2 * width, 1)

    def by_core(values, far, axis):
        core = dp % 2
        size = values.shape[axis] // 2
        own = lax.dynamic_slice_in_dim(values, core * size, size, axis)
        other = lax.dynamic_slice_in_dim(values, (1 - core) * size, size, axis)
        return [swap(own, far) if far else own, swap(other, far ^ 1)]

    def gate_up_term(k, side):
        return mm_tn(side_columns(h_p, k, side), d_both_p)

    def down_term(k, side):
        return mm_tn(act_p, side_columns(g_p, k, side))

    away, here = range(half, outer), range(half)
    near, far = sum_cores(dh_p, dh_a, slab)
    terms = {k: gate_up_term(k, 2).astype(BF) for k in away}
    near, far, terms, d_both_p, act_p = tie(near, far, terms, d_both_p, act_p)
    up_far = send_outer(terms)
    second = exchange(jnp.stack([near[..., cut:], far[..., cut:]], axis=1))
    far = swap(far[..., :cut], 2)
    up_terms = {k: gate_up_term(k, 0).astype(BF) for k in away}
    down_terms = {
        side: {k: down_term(k, side).astype(BF) for k in away} for side in (2, 0)
    }
    first = (near[..., :cut].astype(F32) + far.astype(F32)).astype(BF)
    out_p_terms = down_product(act_p, places, down_pieces)
    second, first, up_terms, down_terms, out_p_terms, up_far, act_p, act_a, d_both_a = tie(
        second, first, up_terms, down_terms, out_p_terms, up_far, act_p, act_a, d_both_a
    )
    down_far, down_close = send_outer(down_terms[2]), send_outer(down_terms[0])
    first = exchange(first)
    second = jnp.sum(second.astype(F32), axis=0)
    second = second[0] + swap(second[1].astype(BF), 2).astype(F32)
    out_near, out_far = sum_cores(out_p_terms, mm(act_a, down_a).astype(BF), slab)
    (first, second, out_near, out_far, down_far, down_close, up_terms) = tie(
        first, second, out_near, out_far, down_far, down_close, up_terms
    )
    act_a, d_both_a, act_p, d_both_p, first = tie(act_a, d_both_a, act_p, d_both_p, first)
    up_close = send_outer(up_terms)
    out_far = swap(out_far, 2)
    dh = jnp.concatenate([jnp.sum(first.astype(F32), axis=0), second], axis=1)
    dh_p, dh_a = unpacked(dh)

    down_grad_a = mm_tn(act_a, g_a).reshape(hidden_a, -1, rows_a).transpose(1, 0, 2)
    small_grad = jnp.concatenate(
        [mm_tn(h_a, d_both_a).reshape(-1, rows_a, 2 * hidden_a), unfold_rows(down_grad_a)],
        axis=2,
    )
    small_terms = {
        k: lax.dynamic_slice_in_dim(small_grad, ((dp // INNER) ^ k) * INNER, INNER, 0)
        for k in range(outer)
    }
    def by_hidden(pieces, hidden):
        value = jnp.zeros((pieces[0].shape[0], INNER * hidden), F32)
        for j, piece in enumerate(pieces):
            place = (inner ^ j) * hidden
            value = lax.dynamic_update_slice_in_dim(value, piece.astype(F32), place, 1)
        return value

    def gate_up_grad(pieces, hidden):
        return jnp.stack(
            [
                by_hidden([p[:, i * hidden : (i + 1) * hidden] for p in pieces], hidden)
                for i in range(2)
            ]
        )

    def down_grad(pieces, hidden):
        value = jnp.zeros((INNER * hidden, pieces[0].shape[1]), F32)
        for j, piece in enumerate(pieces):
            place = (inner ^ j) * hidden
            value = lax.dynamic_update_slice_in_dim(value, piece.astype(F32), place, 0)
        return value

    def tall(piece):
        return jnp.concatenate(
            [piece[:, i : i + rows_a] for i in range(2 * hidden_a, piece.shape[1], rows_a)]
        )

    _, pull_ffn_p = jax.vjp(normed, mid_p, gain_ffn_p)
    from_ffn_p, gain_ffn_grad_p = pull_ffn_p(dh_p)
    d_mid_p = grad_out_p + from_ffn_p
    _, pull_ffn_a = jax.vjp(normed, mid_a, gain_ffn_a)
    from_ffn_a, gain_ffn_grad_a = pull_ffn_a(dh_a)
    d_mid_a = grad_out_a + from_ffn_a

    blocks = spread(packed(d_mid_p, d_mid_a))
    gate_up_far = sum_outer({k: gate_up_term(k, 2) for k in here}, up_far)
    down_far = sum_outer({k: down_term(k, 2) for k in here}, down_far)
    down_close = sum_outer({k: down_term(k, 0) for k in here}, down_close)
    (blocks, gate_up_far, out_far, up_close, d_both_p, gain_ffn_grad_p, gain_ffn_grad_a) = tie(
        blocks, gate_up_far, out_far, up_close, d_both_p, gain_ffn_grad_p, gain_ffn_grad_a
    )
    blocks, down_far, down_close = tie(blocks, down_far, down_close)
    down_got = by_core(down_close, 0, 1) + by_core(down_far, 2, 1)
    out_sums = (out_near.astype(F32) + out_far.astype(F32)).astype(BF)
    out_blocks = [
        lax.dynamic_index_in_dim(out_sums, (z + k) % shard_count, 0, keepdims=False)
        for k in range(shard_count)
    ]
    out_blocks = out_blocks[:1] + [shift(out_blocks[k], k) for k in range(1, shard_count)]
    far_got = by_core(gate_up_far, 2, 0)
    g_mid_p, g_mid_a = unpacked(blocks)
    g_mid_p = g_mid_p.reshape(whole_len, width_p)
    g_mid_a = g_mid_a.reshape(whole_a, width_a)
    d_mixed = jnp.concatenate(
        [
            rows_of_heads(mm_nt(g_mid_p, out_p).astype(BF)),
            rows_of_heads(mm_nt(g_mid_a, out_a).astype(BF)),
        ]
    )
    d_probs = mm_nt(d_mixed, vals)
    d_scores = (probs * (d_probs - jnp.sum(probs * d_probs, axis=-1, keepdims=True))).astype(BF)
    d_query = (mm(d_scores, keys) * scale).astype(BF)
    d_kv = jnp.concatenate(
        [(mm_tn(d_scores, query) * scale).astype(BF), mm_tn(probs_low, d_mixed).astype(BF)], axis=1
    )
    d_all_p = jnp.concatenate([heads_of_rows(d_query[:split], heads_here), d_kv[:whole_len]], axis=1)
    d_all_a = jnp.concatenate([heads_of_rows(d_query[split:], heads_here), d_kv[whole_len:]], axis=1)

    def inner_sum(value, masks):
        lead = [2] * len(masks)
        return dp_scatter(value.reshape(lead + [-1, value.shape[1]]), masks, 1).astype(BF)

    terms_p, terms_a = mm_nt(d_all_p, qkv_p), mm_nt(d_all_a, qkv_a)
    qkv_grad_p = inner_sum(mm_tn(h_attn_p, d_all_p), masks_p)
    gains_terms = jnp.concatenate(
        [gain_ffn_grad_p.reshape(total, -1), gain_ffn_grad_a.reshape(total, -1)], axis=1
    )
    gains_terms = jnp.pad(
        gains_terms[:, None], ((0, 0), (0, 7), (0, width_kv - gains_terms.shape[1]))
    )
    qkv_grad_a = mm_tn(h_attn_a, d_all_a).reshape(total, rows_qa, width_kv)
    qkv_grad_a = jnp.concatenate([qkv_grad_a, gains_terms], axis=1)
    qkv_grad_a = inner_sum(qkv_grad_a.reshape(-1, width_kv), masks_a)
    small_sent = send_outer({k: small_terms[k].astype(BF) for k in away})
    qkv_grad_p, qkv_grad_a, terms_p, terms_a, g_mid_p, d_both_p, small_sent, far_got, out_blocks = (
        tie(
            qkv_grad_p,
            qkv_grad_a,
            terms_p,
            terms_a,
            g_mid_p,
            d_both_p,
            small_sent,
            far_got,
            out_blocks,
        )
    )
    dh_terms = slab_terms(terms_p, terms_a)
    qkv_grad_p = dp_scatter(qkv_grad_p, masks_p[:-1], len(outer_masks))
    qkv_grad_a = dp_scatter(qkv_grad_a, masks_a[:-1], 1)
    out_grad = jnp.concatenate([mm_tn(mixed_p, g_mid_p), mm_tn(mixed_a, g_mid_a)], axis=1)
    out_grad = inner_sum(out_grad, masks_a)
    gate_up_close = sum_outer({k: gate_up_term(k, 0) for k in here}, up_close)
    qkv_grad_p, qkv_grad_a, gate_up_close, out_grad, down_got = tie(
        qkv_grad_p, qkv_grad_a, gate_up_close, out_grad, down_got
    )
    gate_up_got = by_core(gate_up_close, 0, 0) + far_got
    small_grad = sum_outer({k: small_terms[k] for k in here}, small_sent)
    small_got = []
    for j in range(INNER):
        piece = lax.dynamic_index_in_dim(small_grad, inner ^ j, 0, keepdims=False)
        small_got.append(swap(piece, j) if j else piece)
    qkv_grad_p = dp_scatter(qkv_grad_p, masks_p[: -1 - len(outer_masks)])
    qkv_grad_a = dp_scatter(qkv_grad_a, masks_a[:-2])
    out_grad = dp_scatter(out_grad, masks_a[:-1], 1)
    qkv_grad_p, qkv_grad_a, dh_terms, out_grad, small_got, gate_up_got = tie(
        qkv_grad_p, qkv_grad_a, dh_terms, out_grad, small_got, gate_up_got
    )
    by_slab = jnp.concatenate(
        [
            qkv_grad_p.reshape(shard_count, -1, width_kv),
            qkv_grad_a.reshape(shard_count, -1, width_kv),
        ],
        axis=1,
    )
    by_slab = exchange(by_slab.astype(BF)).astype(F32)
    ffn_p, ffn_a = unpacked(sum(block.astype(F32) for block in out_blocks))
    prefix_out = (mid_p + ffn_p).astype(BF)
    action_blocks = ring((mid_a + ffn_a).astype(BF))
    out_grad = dp_scatter(out_grad, masks_a[:-2]).astype(BF)
    out_grad = lax.ppermute(out_grad, everywhere, from_heads).astype(F32)
    dh_attn_p, dh_attn_a = sum_slabs(dh_terms)
    action_out = unring(action_blocks, 0)

    def owned(grad, weights, gains):
        query_part = [grad[k, :, :query_here] for k in range(shard_count)]
        rest = jnp.sum(grad[:, :, query_here:], axis=0)
        whole = jnp.concatenate(query_part + [rest], axis=1)
        return whole * gains, jnp.sum(whole * weights.astype(F32), axis=1)

    qkv_grad_p, gain_attn_grad_p = owned(by_slab[:, :rows_qp], prefix_qkv, own_gain_p)
    qkv_grad_a, gain_attn_grad_a = owned(
        by_slab[:, rows_qp : rows_qp + rows_qa], action_qkv, own_gain_a
    )
    gains_grad = jnp.sum(by_slab[:, rows_qp + rows_qa], axis=0)
    gains_grad_p = jnp.stack([gain_attn_grad_p, gains_grad[:rows_qp]], axis=1)
    gains_grad_a = jnp.stack(
        [gain_attn_grad_a, gains_grad[rows_qp : rows_qp + rows_qa]], axis=1
    )

    _, pull_attn_p = jax.vjp(lambda values: normed(values, 1.0), input_p)
    (from_attn_p,) = pull_attn_p(dh_attn_p)
    _, pull_attn_a = jax.vjp(lambda values: normed(values, 1.0), input_a)
    (from_attn_a,) = pull_attn_a(dh_attn_a)
    action_in_grad = unring(ring(d_mid_a + from_attn_a), 0)

    return (
        prefix_out[None],
        action_out[None, :action_rows],
        (d_mid_p + from_attn_p)[None],
        action_in_grad[None, :action_rows],
        gains_grad_p,
        gains_grad_a,
        qkv_grad_p,
        out_grad[:, :width_p],
        qkv_grad_a,
        out_grad[:, width_p:],
        gate_up_grad(gate_up_got, hidden_p),
        down_grad(down_got, hidden_p),
        gate_up_grad(small_got, hidden_a),
        down_grad([tall(piece) for piece in small_got], hidden_a),
    )


def unfold_rows(values):
    width = values.shape[-1]
    return jnp.concatenate(
        [values[:, i : i + width] for i in range(0, values.shape[1], width)], axis=2
    )


def fold_rows(values, width):
    return jnp.concatenate(
        [values[:, :, i : i + width] for i in range(0, values.shape[2], width)], axis=1
    )


def solution(mesh):
    rows = P(("dp", "mp"), None)
    tokens_p = P("dp", "mp", None)
    tokens_a = P("dp", None, None)
    gate_up = P(None, "dp", "mp")
    down = P("mp", "dp")
    per_item = P("dp")
    in_specs = (
        (tokens_p, tokens_a)
        + (per_item,) * 3
        + (rows,) * 6
        + (gate_up, down, gate_up, down)
        + (tokens_p, tokens_a)
    )
    out_specs = (
        (tokens_p, tokens_a, tokens_p, tokens_a) + (rows,) * 6 + (gate_up, down, gate_up, down)
    )
    return jax.shard_map(
        on_device, mesh=mesh, in_specs=in_specs, out_specs=out_specs, check_vma=False
    )
```

time: 1150 us -> 930 us (0.81)
  matrix products: 213 us -> 80.7 us
  waiting for transfers between devices: 431 us -> 328 us
  Pallas kernels: 0 us -> 66.4 us
  other arithmetic: 162 us -> 136 us
  starting transfers between devices: 174 us -> 159 us
    dot_general x39 -> x29, matrix products: 200 us -> 80.7 us  [dot(): lax.dot_general(left, right, (contract, ((), ())), preferred_element_type...]
    all_to_all x24 -> x11, waiting for transfers between devices: 151 us -> 51.7 us  [exchange(): return lax.all_to_all(value, axes, 0, 0, tiled=True)]
    pallas_call x0 -> x3, Pallas kernels: none -> 66.4 us  [the longest x2 54.7 us: feed_forward(): pl.pallas_call(functools.partial(ffn_kernel, pieces_up=count_up, pieces_d...]
    all_to_all x24 -> x11, starting transfers between devices: 107 us -> 57.1 us  [exchange(): return lax.all_to_all(value, axes, 0, 0, tiled=True)]
    ppermute x37 -> x10, waiting for transfers between devices: 120 us -> 73.1 us  [the longest x9 54.4 us: shift(): lax.ppermute(value, 'mp', [(i, (i + steps) % size) for i in range(size)])]
    ppermute x40 -> x68, waiting for transfers between devices: 160 us -> 195 us  [swap(): return lax.ppermute(value, 'dp', [(i, i ^ mask) for i in range(size)])]
    another operation x18 -> x9, other arithmetic: 41.8 us -> 9.71 us  [the longest x2 4.99 us: gate_up_grad(): jnp.stack([by_hidden([p[:, i * hidden:(i + 1) * hidden] for p in pieces],...]
    ppermute x40 -> x68, starting transfers between devices: 32.1 us -> 60.6 us  [swap(): return lax.ppermute(value, 'dp', [(i, i ^ mask) for i in range(size)])]
  transfers between devices with their start and end apart: 102 -> 90, of which waited for: 35 -> 28; matrix products, arithmetic and copies ran while one was open for 43% -> 31% of each run, Pallas kernels for 0% -> 1%
where the time goes in v2:
time: 930 us; the launch traced here: 922 us
  waiting for transfers between devices  328 us (35%)
  starting transfers between devices  159 us (17%)
  local copies, waits for them, and re-layouts  145 us (16%)
  other arithmetic  136 us (15%)
  matrix products  80.7 us (9%)
  Pallas kernels  66.4 us (7%)
    ppermute x68, waiting for transfers between devices, swap(): return lax.ppermute(value, 'dp', [(i, i ^ mask) for i in range(size)])  195 us
    dot_general x29, matrix products, dot(): lax.dot_general(left, right, (contract, ((), ())), preferred_element_type...  80.7 us
    ppermute x68, starting transfers between devices, swap(): return lax.ppermute(value, 'dp', [(i, i ^ mask) for i in range(size)])  60.6 us
    all_to_all x11, starting transfers between devices, exchange(): return lax.all_to_all(value, axes, 0, 0, tiled=True)  57.1 us
    pallas_call x2, Pallas kernels, feed_forward(): pl.pallas_call(functools.partial(ffn_kernel, pieces_up=count_up, pieces_d...  54.7 us
    ppermute x9, waiting for transfers between devices, shift(): lax.ppermute(value, 'mp', [(i, (i + steps) % size) for i in range(size)])  54.4 us
    all_to_all x11, waiting for transfers between devices, exchange(): return lax.all_to_all(value, axes, 0, 0, tiled=True)  51.7 us
    unnamed x405, local copies, waits for them, and re-layouts  47.1 us
  transfers between devices with their start and end apart: 90, of which 28 were waited for; matrix products, arithmetic and copies ran while one was open for 31% of the time, Pallas kernels for 1%

profile of v2, /device:TPU:4, one launch (start us, length us, event | category | flops | bytes accessed | tf_op | source)
XLA Modules:
  0.0 921.9 jit_solution(4525078810321031650)
XLA Ops:
  24.3 8.5 collective-permute-done
  32.8 9.2 collective-permute-start.4
  44.0 11.2 %all-to-all-start.1 = ((bf16[4,128,2048]{1,2,0:T(8,128)(2,1)}), bf16[4,128,2048]{1,2,0:T(8,128)(2,1)S(1)}, u32[]{:S(2)}, u32[]{:S(2)}) async-start(bf16[4,128,2048]{1,2,0:T(8,128)(2,1)} %broadcast_in_dim.371), calls=%async_computation.1 | async-start | bytes 4194304 | tf_op jit(solution)/shard_map/all_to_all | solution.py:89
  64.9 9.5 %collective-permute-done.1 = bf16[256,1024]{1,0:T(8,128)(2,1)S(1)} collective-permute-done((bf16[256,1024]{1,0:T(8,128)(2,1)S(1)}, bf16[256,1024]{1,0:T(8,128)(2,1)S(1)}, u32[]{:S(2)}, u32[]{:S(2)}) %collective-permute-start.1) | collective-permute-done | bytes 524320 | tf_op jit(solution)/shard_map/ppermute | solution.py:52
  146.0 17.2 %collective-permute-done.11 = bf16[256,4096]{1,0:T(8,128)(2,1)} collective-permute-done((bf16[256,4096]{1,0:T(8,128)(2,1)}, bf16[256,4096]{1,0:T(8,128)(2,1)}, u32[]{:S(2)}, u32[]{:S(2)}) %collective-permute-start.11) | collective-permute-done | bytes 2097184 | tf_op jit(solution)/shard_map/ppermute | solution.py:52
  164.9 10.4 %all-to-all-done.2 = bf16[4,136,2048]{2,1,0:T(8,128)(2,1)} async-done(((bf16[4,136,2048]{2,1,0:T(8,128)(2,1)}), bf16[4,136,2048]{2,1,0:T(8,128)(2,1)}, u32[]{:S(2)}, u32[]{:S(2)}) %all-to-all-start.2) | async-done | bytes 2228256 | tf_op jit(solution)/shard_map/all_to_all | solution.py:89
  201.9 35.0 %all-to-all-done.3 = bf16[4,136,2048]{2,1,0:T(8,128)(2,1)} async-done(((bf16[4,136,2048]{2,1,0:T(8,128)(2,1)}), bf16[4,136,2048]{2,1,0:T(8,128)(2,1)}, u32[]{:S(2)}, u32[]{:S(2)}) %all-to-all-start.3) | async-done | bytes 2228256 | tf_op jit(solution)/shard_map/all_to_all | solution.py:89
  317.8 20.7 %collective-permute-done.28 = bf16[4,136,1280]{2,1,0:T(8,128)(2,1)} collective-permute-done((bf16[4,136,1280]{2,1,0:T(8,128)(2,1)}, bf16[4,136,1280]{2,1,0:T(8,128)(2,1)}, u32[]{:S(2)}, u32[]{:S(2)}) %collective-permute-start.28) | collective-permute-done | bytes 1392672 | tf_op jit(solution)/shard_map/ppermute | solution.py:52
  361.5 52.7 %ffn.2 = (bf16[2048,1024]{1,0:T(8,128)(2,1)}, bf16[2048,2048]{1,0:T(8,128)(2,1)}, bf16[2048,2048]{1,0:T(8,128)(2,1)}) custom-call(s32[8]{0:T(128)S(1)} %iota_xor_fusion.places_ref, bf16[2048,2048]{1,0:T(8,128)(2,1)} %pad_maximum_fusion.1.h_ref, bf16[2048,2048]{1,0:T(8,128)(2,1)} %pad_maximum_fusion.g_ref, bf16[256,2048]{1,0:T(8,128)(2,1)S(1)} %copy-done.3, ...), custom_call_target="tpu_custom_call" | custom-call | tf_op jit(solution)/shard_map/ffn/pallas_call | solution.py:200
  424.5 10.1 %convolution_convert_fusion.1 = bf16[512,2048]{1,0:T(8,128)(2,1)} fusion(bf16[2048,2048]{1,0:T(8,128)(2,1)} %get-tuple-element.238, bf16[2048,2048]{1,0:T(8,128)(2,1)} %pad_maximum_fusion.1.h_ref, s32[]{:T(128)S(6)} %select_n.446), kind=kOutput, calls=%fused_computation.33 | convolution fusion | flops 4296015872 | bytes 12582916 | tf_op jit(solution)/shard_map/dot_general | solution.py:22
  458.4 11.8 %down.1 = bf16[2048,2048]{1,0:T(8,128)(2,1)S(1)} custom-call(s32[8]{0:T(128)S(1)} %iota_xor_fusion.places_ref, bf16[2048,1024]{1,0:T(8,128)(2,1)S(1)} %copy-done.1, bf16[1024,256]{1,0:T(8,128)(2,1)S(1)} %get-tuple-element.354.refs_8_.refs_0_, bf16[1024,256]{1,0:T(8,128)(2,1)S(1)} %collective-permute-done.31.refs_9_.refs_1_, ...), custom_call_target="tpu_custom_call" | custom-call | tf_op jit(solution)/shard_map/down/pallas_call | solution.py:237
  487.3 17.0 %collective-permute-done.42 = bf16[512,2048]{1,0:T(8,128)(2,1)} collective-permute-done((bf16[512,2048]{1,0:T(8,128)(2,1)S(1)}, bf16[512,2048]{1,0:T(8,128)(2,1)}, u32[]{:S(2)}, u32[]{:S(2)}) %collective-permute-start.42) | collective-permute-done | bytes 2097184 | tf_op jit(solution)/shard_map/ppermute | solution.py:52
  543.3 14.9 %collective-permute-done.46 = bf16[1024,512]{1,0:T(8,128)(2,1)S(1)} collective-permute-done((bf16[1024,512]{1,0:T(8,128)(2,1)S(1)}, bf16[1024,512]{1,0:T(8,128)(2,1)S(1)}, u32[]{:S(2)}, u32[]{:S(2)}) %collective-permute-start.46) | collective-permute-done | bytes 1048608 | tf_op jit(solution)/shard_map/ppermute | solution.py:52
  559.1 20.3 %collective-permute-done.47 = bf16[1024,512]{1,0:T(8,128)(2,1)} collective-permute-done((bf16[1024,512]{1,0:T(8,128)(2,1)S(1)}, bf16[1024,512]{1,0:T(8,128)(2,1)}, u32[]{:S(2)}, u32[]{:S(2)}) %collective-permute-start.47) | collective-permute-done | bytes 1048608 | tf_op jit(solution)/shard_map/ppermute | solution.py:52
  617.5 23.4 %collective-permute-done.49 = bf16[512,2048]{1,0:T(8,128)(2,1)} collective-permute-done((bf16[512,2048]{1,0:T(8,128)(2,1)}, bf16[512,2048]{1,0:T(8,128)(2,1)}, u32[]{:S(2)}, u32[]{:S(2)}) %collective-permute-start.49) | collective-permute-done | bytes 2097184 | tf_op jit(solution)/shard_map/ppermute | solution.py:52
  692.6 23.2 %collective-permute-done.56 = bf16[136,2048]{1,0:T(8,128)(2,1)S(1)} collective-permute-done((bf16[136,2048]{1,0:T(8,128)(2,1)S(1)}, bf16[136,2048]{1,0:T(8,128)(2,1)S(1)}, u32[]{:S(2)}, u32[]{:S(2)}) %collective-permute-start.56) | collective-permute-done | bytes 557088 | tf_op jit(solution)/shard_map/ppermute | solution.py:98
  720.5 13.1 %collective-permute-start.58 = (bf16[16,1024]{1,0:T(8,128)(2,1)S(1)}, bf16[16,1024]{1,0:T(8,128)(2,1)S(1)}, u32[]{:S(2)}, u32[]{:S(2)}) collective-permute-start(bf16[16,1024]{1,0:T(8,128)(2,1)S(1)} %get-tuple-element.279), channel_id=1, source_target_pairs={{0,3},{1,0},{2,1},{3,2},{4,7},{5,4},{6,5},{7,6},{8,11},{9,8},{10,9... | collective-permute-start | bytes 98312 | tf_op jit(solution)/shard_map/ppermute | solution.py:98
  746.9 9.3 %add_convert_fusion.5 = bf16[512,2048]{1,0:T(8,128)(2,1)S(1)} fusion(bf16[512,2048]{1,0:T(8,128)(2,1)} %collective-permute-done.49, bf16[2048,2048]{1,0:T(8,128)(2,1)} %get-tuple-element.238, bf16[2048,2048]{1,0:T(8,128)(2,1)} %pad_maximum_fusion.1.h_ref, s32[]{:T(128)S(6)} %select_n.451), kind=kOutput, calls=%fused_computation.18 | convolution fusion | flops 4298113024 | bytes 14680068 | tf_op jit(solution)/shard_map/dot_general | solution.py:22
  762.3 24.6 %collective-permute-done.60 = bf16[16,1024]{1,0:T(8,128)(2,1)S(1)} collective-permute-done((bf16[16,1024]{1,0:T(8,128)(2,1)S(1)}, bf16[16,1024]{1,0:T(8,128)(2,1)S(1)}, u32[]{:S(2)}, u32[]{:S(2)}) %collective-permute-start.60) | collective-permute-done | bytes 32800 | tf_op jit(solution)/shard_map/ppermute | solution.py:98
  789.3 13.3 %collective-permute-done.62 = bf16[2,160,1024]{2,1,0:T(8,128)(2,1)S(1)} collective-permute-done((bf16[2,160,1024]{2,1,0:T(8,128)(2,1)S(1)}, bf16[2,160,1024]{2,1,0:T(8,128)(2,1)S(1)}, u32[]{:S(2)}, u32[]{:S(2)}) %collective-permute-start.62) | collective-permute-done | bytes 655392 | tf_op jit(solution)/shard_map/ppermute | solution.py:52
  807.5 9.1 collective-permute-done.66
  833.9 15.5 %collective-permute-done.69 = bf16[2,64,3072]{2,1,0:T(8,128)(2,1)S(1)} collective-permute-done((bf16[2,64,3072]{2,1,0:T(8,128)(2,1)S(1)}, bf16[2,64,3072]{2,1,0:T(8,128)(2,1)S(1)}, u32[]{:S(2)}, u32[]{:S(2)}) %collective-permute-start.69) | collective-permute-done | bytes 786464 | tf_op jit(solution)/shard_map/ppermute | solution.py:52
  856.5 11.5 %collective-permute-start.75 = (f32[16,1024]{1,0:T(8,128)}, f32[16,1024]{1,0:T(8,128)}, u32[]{:S(2)}, u32[]{:S(2)}) collective-permute-start(f32[16,1024]{1,0:T(8,128)} %get-tuple-element.277), channel_id=1, source_target_pairs={{0,2},{1,3},{2,0},{3,1},{4,6},{5,7},{6,4},{7,5},{8,10},{9,11},{10,... | collective-permute-start | bytes 196616 | tf_op jit(solution)/shard_map/ppermute | solution.py:98
  897.2 18.7 %collective-permute-done.78 = bf16[64,3072]{1,0:T(8,128)(2,1)S(1)} collective-permute-done((bf16[64,3072]{1,0:T(8,128)(2,1)S(1)}, bf16[64,3072]{1,0:T(8,128)(2,1)S(1)}, u32[]{:S(2)}, u32[]{:S(2)}) %collective-permute-start.78) | collective-permute-done | bytes 393248 | tf_op jit(solution)/shard_map/ppermute | solution.py:717
  (890 shorter events, 505.4 us)
Async XLA Ops:
  17.5 47.4 %collective-permute-start.2 = (bf16[2048,256]{1,0:T(8,128)(2,1)}, bf16[2048,256]{1,0:T(8,128)(2,1)}, u32[]{:S(2)}, u32[]{:S(2)}) collective-permute-start(bf16[2048,256]{1,0:T(8,128)(2,1)} %get-tuple-element.322), channel_id=1, source_target_pairs={{0,8},{4,12},{8,0},{12,4},{16,24},{20,28},{24,16},{28,20},{1,9},{5... | collective-permute-start | bytes 3145736 | tf_op jit(solution)/shard_map/ppermute | solution.py:52
  44.0 65.6 %all-to-all-start.1 = ((bf16[4,128,2048]{1,2,0:T(8,128)(2,1)}), bf16[4,128,2048]{1,2,0:T(8,128)(2,1)S(1)}, u32[]{:S(2)}, u32[]{:S(2)}) async-start(bf16[4,128,2048]{1,2,0:T(8,128)(2,1)} %broadcast_in_dim.371), calls=%async_computation.1 | async-start | bytes 4194304 | tf_op jit(solution)/shard_map/all_to_all | solution.py:89
  115.1 48.2 %collective-permute-start.11 = (bf16[256,4096]{1,0:T(8,128)(2,1)}, bf16[256,4096]{1,0:T(8,128)(2,1)}, u32[]{:S(2)}, u32[]{:S(2)}) collective-permute-start(bf16[256,4096]{1,0:T(8,128)(2,1)} %pad_maximum_fusion.9), channel_id=1, source_target_pairs={{0,8},{4,12},{8,0},{12,4},{16,24},{20,28},{24,16},{28,20},{1,9},{5... | collective-permute-start | bytes 6291464 | tf_op jit(solution)/shard_map/ppermute | solution.py:52
  117.1 47.9 %collective-permute-start.12 = (bf16[256,4096]{1,0:T(8,128)(2,1)}, bf16[256,4096]{1,0:T(8,128)(2,1)}, u32[]{:S(2)}, u32[]{:S(2)}) collective-permute-start(bf16[256,4096]{1,0:T(8,128)(2,1)} %pad_maximum_fusion.10), channel_id=1, source_target_pairs={{0,16},{4,20},{8,24},{12,28},{16,0},{20,4},{24,8},{28,12},{1,17},{... | collective-permute-start | bytes 6291464 | tf_op jit(solution)/shard_map/ppermute | solution.py:52
  119.3 56.1 %all-to-all-start.2 = ((bf16[4,136,2048]{2,1,0:T(8,128)(2,1)}), bf16[4,136,2048]{2,1,0:T(8,128)(2,1)}, u32[]{:S(2)}, u32[]{:S(2)}) async-start(bf16[4,136,2048]{2,1,0:T(8,128)(2,1)} %broadcast_in_dim.386), calls=%async_computation.2 | async-start | bytes 4456448 | tf_op jit(solution)/shard_map/all_to_all | solution.py:89
  181.6 55.3 %all-to-all-start.3 = ((bf16[4,136,2048]{2,1,0:T(8,128)(2,1)}), bf16[4,136,2048]{2,1,0:T(8,128)(2,1)}, u32[]{:S(2)}, u32[]{:S(2)}) async-start(bf16[4,136,2048]{2,1,0:T(8,128)(2,1)} %maximum_maximum_fusion), calls=%async_computation.3 | async-start | bytes 4456448 | tf_op jit(solution)/shard_map/all_to_all | solution.py:89
  199.0 73.6 %collective-permute-start.18 = (bf16[4,136,2048]{2,1,0:T(8,128)(2,1)}, bf16[4,136,2048]{2,1,0:T(8,128)(2,1)}, u32[]{:S(2)}, u32[]{:S(2)}) collective-permute-start(bf16[4,136,2048]{2,1,0:T(8,128)(2,1)} %all-to-all-done.2), channel_id=1, source_target_pairs={{0,8},{4,12},{8,0},{12,4},{16,24},{20,28},{24,16},{28,20},{1,9},{5... | collective-permute-start | bytes 6684680 | tf_op jit(solution)/shard_map/ppermute | solution.py:52
  199.3 57.8 %collective-permute-start.20 = (bf16[4,136,2048]{2,1,0:T(8,128)(2,1)}, bf16[4,136,2048]{2,1,0:T(8,128)(2,1)}, u32[]{:S(2)}, u32[]{:S(2)}) collective-permute-start(bf16[4,136,2048]{2,1,0:T(8,128)(2,1)} %all-to-all-done.2), channel_id=1, source_target_pairs={{0,4},{4,0},{8,12},{12,8},{16,20},{20,16},{24,28},{28,24},{1,5},{5... | collective-permute-start | bytes 6684680 | tf_op jit(solution)/shard_map/ppermute | solution.py:52
  199.3 72.6 %collective-permute-start.17 = (bf16[256,4096]{1,0:T(8,128)(2,1)}, bf16[256,4096]{1,0:T(8,128)(2,1)}, u32[]{:S(2)}, u32[]{:S(2)}) collective-permute-start(bf16[256,4096]{1,0:T(8,128)(2,1)} %collective-permute-done.11), channel_id=1, source_target_pairs={{0,16},{4,20},{8,24},{12,28},{16,0},{20,4},{24,8},{28,12},{1,17},{... | collective-permute-start | bytes 6291464 | tf_op jit(solution)/shard_map/ppermute | solution.py:52
  253.0 57.1 %collective-permute-start.22 = (bf16[256,2048]{1,0:T(8,128)(2,1)}, bf16[256,2048]{1,0:T(8,128)(2,1)S(1)}, u32[]{:S(2)}, u32[]{:S(2)}) collective-permute-start(bf16[256,2048]{1,0:T(8,128)(2,1)} %get-tuple-element.315), channel_id=1, source_target_pairs={{0,4},{4,0},{8,12},{12,8},{16,20},{20,16},{24,28},{28,24},{1,5},{5... | collective-permute-start | bytes 3145736 | tf_op jit(solution)/shard_map/ppermute | solution.py:52
  281.5 57.1 %all-to-all-start.5 = ((bf16[4,2,136,768]{3,2,1,0:T(8,128)(2,1)}), bf16[4,2,136,768]{3,2,1,0:T(8,128)(2,1)}, u32[]{:S(2)}, u32[]{:S(2)}) async-start(bf16[4,2,136,768]{3,2,1,0:T(8,128)(2,1)} %broadcast_in_dim.395), calls=%async_computation.5 | async-start | bytes 3342336 | tf_op jit(solution)/shard_map/all_to_all | solution.py:89
  443.6 60.7 %all-to-all-start.6 = ((bf16[4,2,136,768]{3,2,1,0:T(8,128)(2,1)}), bf16[4,2,136,768]{3,2,1,0:T(8,128)(2,1)}, u32[]{:S(2)}, u32[]{:S(2)}) async-start(bf16[4,2,136,768]{3,2,1,0:T(8,128)(2,1)} %pad_maximum_fusion.11), calls=%async_computation.6 | async-start | bytes 3342336 | tf_op jit(solution)/shard_map/all_to_all | solution.py:89
  514.2 65.2 %all-to-all-start.7 = ((bf16[4,136,1280]{2,1,0:T(8,128)(2,1)}), bf16[4,136,1280]{2,1,0:T(8,128)(2,1)}, u32[]{:S(2)}, u32[]{:S(2)}) async-start(bf16[4,136,1280]{2,1,0:T(8,128)(2,1)} %add_convert_fusion.7), calls=%async_computation.7 | async-start | bytes 2785280 | tf_op jit(solution)/shard_map/all_to_all | solution.py:89
  585.5 55.4 %all-to-all-start.8 = ((bf16[4,136,2048]{2,1,0:T(8,128)(2,1)}), bf16[4,136,2048]{2,1,0:T(8,128)(2,1)}, u32[]{:S(2)}, u32[]{:S(2)}) async-start(bf16[4,136,2048]{2,1,0:T(8,128)(2,1)} %broadcast_in_dim.398), calls=%async_computation.8 | async-start | bytes 4456448 | tf_op jit(solution)/shard_map/all_to_all | solution.py:89
  590.3 50.6 %collective-permute-start.48 = (bf16[4,136,2048]{2,1,0:T(8,128)(2,1)}, bf16[4,136,2048]{2,1,0:T(8,128)(2,1)}, u32[]{:S(2)}, u32[]{:S(2)}) collective-permute-start(bf16[4,136,2048]{2,1,0:T(8,128)(2,1)} %add_convert_fusion.1), channel_id=1, source_target_pairs={{0,8},{4,12},{8,0},{12,4},{16,24},{20,28},{24,16},{28,20},{1,9},{5... | collective-permute-start | bytes 6684680 | tf_op jit(solution)/shard_map/ppermute | solution.py:52
  592.0 48.9 %collective-permute-start.49 = (bf16[512,2048]{1,0:T(8,128)(2,1)}, bf16[512,2048]{1,0:T(8,128)(2,1)}, u32[]{:S(2)}, u32[]{:S(2)}) collective-permute-start(bf16[512,2048]{1,0:T(8,128)(2,1)} %convolution_convert_fusion), channel_id=1, source_target_pairs={{0,16},{4,20},{8,24},{12,28},{16,0},{20,4},{24,8},{28,12},{1,17},{... | collective-permute-start | bytes 6291464 | tf_op jit(solution)/shard_map/ppermute | solution.py:52
  595.7 79.4 %collective-permute-start.52 = (bf16[4,128,768]{2,1,0:T(8,128)(2,1)S(1)}, bf16[4,128,768]{2,1,0:T(8,128)(2,1)}, u32[]{:S(2)}, u32[]{:S(2)}) collective-permute-start(bf16[4,128,768]{2,1,0:T(8,128)(2,1)S(1)} %dynamic-slice_convert_fusion.1), channel_id=1, source_target_pairs={{0,16},{4,20},{8,24},{12,28},{16,0},{20,4},{24,8},{28,12},{1,17},{... | collective-permute-start | bytes 2359304 | tf_op jit(solution)/shard_map/ppermute | solution.py:52
  663.6 53.0 %collective-permute-start.53 = (bf16[256,2048]{1,0:T(8,128)(2,1)S(1)}, bf16[256,2048]{1,0:T(8,128)(2,1)S(1)}, u32[]{:S(2)}, u32[]{:S(2)}) collective-permute-start(bf16[256,2048]{1,0:T(8,128)(2,1)S(1)} %get-tuple-element.308), channel_id=1, source_target_pairs={{0,8},{4,12},{8,0},{12,4},{16,24},{20,28},{24,16},{28,20},{1,9},{5... | collective-permute-start | bytes 3145736 | tf_op jit(solution)/shard_map/ppermute | solution.py:52
  664.5 52.1 %collective-permute-start.54 = (bf16[256,2048]{1,0:T(8,128)(2,1)S(1)}, bf16[256,2048]{1,0:T(8,128)(2,1)S(1)}, u32[]{:S(2)}, u32[]{:S(2)}) collective-permute-start(bf16[256,2048]{1,0:T(8,128)(2,1)S(1)} %get-tuple-element.307), channel_id=1, source_target_pairs={{0,12},{4,8},{8,4},{12,0},{16,28},{20,24},{24,20},{28,16},{1,13},{... | collective-permute-start | bytes 3145736 | tf_op jit(solution)/shard_map/ppermute | solution.py:52
  692.6 114.9 %collective-permute-start.64 = (bf16[1024,256]{1,0:T(8,128)(2,1)}, bf16[1024,256]{1,0:T(8,128)(2,1)}, u32[]{:S(2)}, u32[]{:S(2)}) collective-permute-start(bf16[1024,256]{1,0:T(8,128)(2,1)} %get-tuple-element.343), channel_id=1, source_target_pairs={{0,4},{4,0},{8,12},{12,8},{16,20},{20,16},{24,28},{28,24},{1,5},{5... | collective-permute-start | bytes 1572872 | tf_op jit(solution)/shard_map/ppermute | solution.py:52
  715.8 91.7 %collective-permute-start.65 = (bf16[1024,256]{1,0:T(8,128)(2,1)}, bf16[1024,256]{1,0:T(8,128)(2,1)}, u32[]{:S(2)}, u32[]{:S(2)}) collective-permute-start(bf16[1024,256]{1,0:T(8,128)(2,1)} %get-tuple-element.342), channel_id=1, source_target_pairs={{0,8},{4,12},{8,0},{12,4},{16,24},{20,28},{24,16},{28,20},{1,9},{5... | collective-permute-start | bytes 1572872 | tf_op jit(solution)/shard_map/ppermute | solution.py:52
  739.6 65.5 %collective-permute-start.63 = (bf16[2,2,64,3072]{3,2,0,1:T(8,128)(2,1)}, bf16[2,2,64,3072]{3,2,0,1:T(8,128)(2,1)}, u32[]{:S(2)}, u32[]{:S(2)}) collective-permute-start(bf16[2,2,64,3072]{3,2,0,1:T(8,128)(2,1)} %fusion.31), channel_id=1, source_target_pairs={{0,4},{4,0},{8,12},{12,8},{16,20},{20,16},{24,28},{28,24},{1,5},{5... | collective-permute-start | bytes 4718600 | tf_op jit(solution)/shard_map/ppermute | solution.py:52
  741.2 112.6 %all-to-all-start.9 = ((bf16[4,136,2048]{2,1,0:T(8,128)(2,1)}), bf16[4,136,2048]{2,1,0:T(8,128)(2,1)S(1)}, u32[]{:S(2)}, u32[]{:S(2)}) async-start(bf16[4,136,2048]{2,1,0:T(8,128)(2,1)} %maximum_maximum_fusion.1), calls=%async_computation.9 | async-start | bytes 4456448 | tf_op jit(solution)/shard_map/all_to_all | solution.py:89
  802.9 47.9 %collective-permute-start.70 = (bf16[128,768]{1,0:T(8,128)(2,1)S(1)}, bf16[128,768]{1,0:T(8,128)(2,1)S(1)}, u32[]{:S(2)}, u32[]{:S(2)}) collective-permute-start(bf16[128,768]{1,0:T(8,128)(2,1)S(1)} %get-tuple-element.367), channel_id=1, source_target_pairs={{0,4},{4,0},{8,12},{12,8},{16,20},{20,16},{24,28},{28,24},{1,5},{5... | collective-permute-start | bytes 589832 | tf_op jit(solution)/shard_map/ppermute | solution.py:52
  (249 other events, 3080.5 us)
